TPU v7x, 128 devices: a whole 4x4x4 slice. The times are simulated.
128 devices in a mesh: dom: 128 (over z, x, y, core).
Axes of the slice: x: 4, y: 4, z: 4, core: 2. Of those that a mesh axis runs over, the one named last changes fastest.
Arguments:
- state: float32 [6144, 2048], P('dom'), may hold values from -6 to 6
- cotangent: float32 [6144, 2048], P('dom'), may hold values from -6 to 6
- elem_count: int32 [128], P('dom'), may hold values from 24 to 48, as said below
- face_src: int32 [36864], P('dom'), may hold values from 0 to 543, as said below
- face_orient: int32 [36864], P('dom'), may hold values from 0 to 7
- send_face: int32 [32768], P('dom'), may hold values from -1 to 287, as said below
- vol_weight: float32 [2, 3, 32, 32], replicated, may hold values from -0.15625 to 0.15625
- flux_w1: float32 [2, 64, 64], replicated, may hold values from -0.75 to 0.75
- flux_b1: float32 [2, 64], replicated, may hold values from -3 to 3
- flux_w2: float32 [2, 64, 32], replicated, may hold values from -0.75 to 0.75
Outputs:
- grad_state: float32 [6144, 2048], P('dom')
- grad_w1: float32 [2, 64, 64], replicated
- grad_b1: float32 [2, 64], replicated
- grad_w2: float32 [2, 64, 32], replicated
Inputs may be any that keep to these rules, and one draw needn't show every extreme that they name: `elem_count`: one partition holds exactly 48 live elements; the others at least half of that. `send_face`: Partitions at offsets 1 and 4 share exactly 32 faces where they exist; the counts are symmetric between two partitions. `face_src`: A value of 288 or more always names a slot that its sender fills, and the face it appears on is the face that the partition sends into the mirrored slot; faces are otherwise paired within the partition or are their own partners.
All inputs are finite; a program needn't handle non-finite values.
Results may differ from a plain program's by a relative error of at most 0.00011.
Values sent between devices are 32-bit elements; how exact they have to be, the bound alone decides.
A program may use at most 128 MiB of HBM per device.

v0:
```python
import jax
import jax.numpy as jnp
import numpy as np
from jax import lax
from jax.sharding import PartitionSpec as P

NEIGH = 4


HIGHEST = lax.Precision.HIGHEST
STEP_SIZE = 0.25


def shifted(value, axis, steps):
    count = lax.axis_size(axis)
    initial, last = (max(0, -steps), min(count, count - steps))
    return lax.ppermute(value, axis, [(source, source + steps) for source in range(initial, last)])


def neighbour_offsets():
    return [level + 1 for level in range(NEIGH)] + [-(level + 1) for level in range(NEIGH)]


def face_nodes():
    table = np.zeros((6, 16), np.int32)
    for facet in range(6):
        fixed_value = 0 if facet % 2 == 0 else 3
        for first in range(4):
            for second in range(4):
                if facet < 2:
                    coords = (fixed_value, first, second)
                elif facet < 4:
                    coords = (first, fixed_value, second)
                else:
                    coords = (first, second, fixed_value)
                table[facet, 4 * first + second] = 16 * coords[0] + 4 * coords[1] + coords[2]
    return table


def select_matrix():
    matrix = np.zeros((96, 64), np.float32)
    nodes = face_nodes()
    for facet in range(6):
        for member in range(16):
            matrix[16 * facet + member, nodes[facet, member]] = 1.0
    return matrix


def orient_table():
    table = np.zeros((8, 16), np.int32)
    for variant in range(8):
        for member in range(16):
            first, second = (member // 4, member % 4)
            if variant >= 4:
                first, second = (second, first)
            for turn in range(variant % 4):
                first, second = (second, 3 - first)
            table[variant, member] = 4 * first + second
    return table


def deriv_matrix():
    points = np.array([-1.0, -np.sqrt(0.2), np.sqrt(0.2), 1.0])
    weights = np.array(
        [
            np.prod([points[row_at] - points[other] for other in range(4) if other != row_at])
            for row_at in range(4)
        ]
    )
    matrix = np.zeros((4, 4))
    for row_at in range(4):
        for column in range(4):
            if row_at != column:
                matrix[row_at, column] = (
                    weights[row_at] / weights[column] / (points[row_at] - points[column])
                )
        matrix[row_at, row_at] = -np.sum(matrix[row_at])
    return matrix


def orient_index(face_orient):
    table = jnp.asarray(orient_table(), jnp.int32)
    match = face_orient[:, None] == jnp.arange(8, dtype=jnp.int32)[None, :]
    return jnp.sum(jnp.where(match[:, :, None], table[None, :, :], 0), axis=1)


def face_traces(field):
    row_count = field.shape[0]
    width = field.shape[1] // 64
    select = jnp.asarray(select_matrix(), jnp.float32)
    nodes = field.reshape(row_count, 64, width)
    return jnp.einsum("qn,enc->eqc", select, nodes, precision=HIGHEST).reshape(
        row_count * 6, 16 * width
    )


def trace_adjoint(grad_inner, row_count):
    width = grad_inner.shape[1] // 16
    select = jnp.asarray(select_matrix(), jnp.float32)
    tiles = grad_inner.reshape(row_count, 96, width)
    return jnp.einsum("qn,eqc->enc", select, tiles, precision=HIGHEST).reshape(
        row_count, 64 * width
    )


def outer_traces(pool, source_rows, orient_rows):
    width = pool.shape[1] // 16
    tiles = pool[source_rows].reshape(-1, 16, width)
    turned = jnp.take_along_axis(tiles, orient_rows[:, :, None], axis=1)
    return turned.reshape(-1, 16 * width)


def pack_tiles(inner, send_face):
    position = jnp.clip(send_face, 0, inner.shape[0] - 1)
    return jnp.where((send_face >= 0)[:, None], inner[position], 0.0)


def flux_step(field, inner, outer, vol_w, weight_one, bias_one, weight_two):
    row_count = field.shape[0]
    width = weight_two.shape[1]
    deriv = jnp.asarray(deriv_matrix(), jnp.float32)
    select = jnp.asarray(select_matrix(), jnp.float32)
    cube = field.reshape(row_count, 4, 4, 4, width)
    along_i = jnp.einsum("ai,eijkc->eajkc", deriv, cube, precision=HIGHEST)
    along_j = jnp.einsum("aj,eijkc->eiakc", deriv, cube, precision=HIGHEST)
    along_k = jnp.einsum("ak,eijkc->eijac", deriv, cube, precision=HIGHEST)
    volume = jnp.einsum("eijkc,cd->eijkd", along_i, vol_w[0], precision=HIGHEST)
    volume = volume + jnp.einsum("eijkc,cd->eijkd", along_j, vol_w[1], precision=HIGHEST)
    volume = volume + jnp.einsum("eijkc,cd->eijkd", along_k, vol_w[2], precision=HIGHEST)
    inner_rows = inner.reshape(-1, width)
    outer_rows = outer.reshape(-1, width)
    hidden = jnp.tanh(
        jnp.dot(inner_rows, weight_one[:width], precision=HIGHEST)
        + jnp.dot(outer_rows, weight_one[width:], precision=HIGHEST)
        + bias_one
    )
    flux = jnp.dot(hidden, weight_two, precision=HIGHEST).reshape(row_count, 96, width)
    lifted = jnp.einsum("qn,eqc->enc", select, flux, precision=HIGHEST)
    change = lifted - volume.reshape(row_count, 64, width)
    return field + STEP_SIZE * change.reshape(row_count, 64 * width)


def local(
    state,
    cotangent,
    elem_count,
    face_src,
    face_orient,
    send_face,
    vol_weight,
    flux_w1,
    flux_b1,
    flux_w2,
):
    row_count = state.shape[0]
    layer_count = flux_w1.shape[0]
    slot_count = send_face.shape[0]
    block_count = 2 * NEIGH
    capacity = slot_count // block_count
    tile_width = 16 * (state.shape[1] // 64)
    offsets = neighbour_offsets()
    device_count = lax.axis_size("dom")
    alive_mask = (jnp.arange(row_count, dtype=jnp.int32) < elem_count[0]).astype(jnp.float32)[
        :, None
    ]
    orient_rows = orient_index(face_orient)

    def deliver(sent):
        blocks = sent.reshape(block_count, capacity, tile_width)
        fetched = jnp.stack(
            [shifted(blocks[block], "dom", offsets[block]) for block in range(block_count)]
        )
        return fetched.reshape(slot_count, tile_width)

    def give_back(grad_received):
        blocks = grad_received.reshape(block_count, capacity, tile_width)
        fetched = jnp.stack(
            [shifted(blocks[block], "dom", -offsets[block]) for block in range(block_count)]
        )
        return fetched.reshape(slot_count, tile_width)

    field = state * alive_mask
    stored = []
    for layer in range(layer_count):
        inner = face_traces(field)
        received = deliver(pack_tiles(inner, send_face))
        outer = outer_traces(jnp.concatenate([inner, received], axis=0), face_src, orient_rows)
        stored.append((field, inner, received, outer))
        field = flux_step(
            field, inner, outer, vol_weight[layer], flux_w1[layer], flux_b1[layer], flux_w2[layer]
        )
    grad_field = cotangent
    summed = [None] * layer_count
    for layer in reversed(range(layer_count)):
        old_field, inner, received, outer = stored[layer]
        layer_vol = vol_weight[layer]

        def layer_step(field_in, inner_in, outer_in, weight_one, bias_one, weight_two):
            return flux_step(
                field_in, inner_in, outer_in, layer_vol, weight_one, bias_one, weight_two
            )

        result_now, step_back = jax.vjp(
            layer_step, old_field, inner, outer, flux_w1[layer], flux_b1[layer], flux_w2[layer]
        )
        grad_old, grad_inner, grad_outer, grad_one, grad_bias, grad_two = step_back(grad_field)

        def build_outer(inner_in, received_in):
            return outer_traces(
                jnp.concatenate([inner_in, received_in], axis=0), face_src, orient_rows
            )

        result_outer, outer_back = jax.vjp(build_outer, inner, received)
        grad_inner_local, grad_received = outer_back(grad_outer)
        grad_sent = give_back(grad_received)
        result_pack, pack_back = jax.vjp(lambda inner_in: pack_tiles(inner_in, send_face), inner)
        (grad_inner_sent,) = pack_back(grad_sent)
        grad_inner_all = grad_inner + grad_inner_local + grad_inner_sent
        grad_field = grad_old + trace_adjoint(grad_inner_all, row_count)
        summed[layer] = lax.psum((grad_one, grad_bias, grad_two), "dom")
    total_one = jnp.stack([item[0] for item in summed])
    total_bias = jnp.stack([item[1] for item in summed])
    total_two = jnp.stack([item[2] for item in summed])
    factor = (96.0 * row_count * device_count) ** (-0.5)
    return (grad_field * alive_mask, total_one * factor, total_bias * factor, total_two * factor)


def solution(mesh):
    placed = (
        P("dom", None),
        P("dom", None),
        P("dom"),
        P("dom"),
        P("dom"),
        P("dom"),
        P(),
        P(),
        P(),
        P(),
    )
    return jax.shard_map(
        local,
        mesh=mesh,
        in_specs=placed,
        out_specs=(P("dom", None), P(), P(), P()),
        check_vma=False,
    )
```

profile of v0, /device:TPU:30, one launch (start us, length us, event | category | flops | bytes accessed | tf_op | source)
XLA Modules:
  0.0 619.2 jit_solution(832748201473877819)
XLA Ops:
  45.6 5.3 fusion.32
  68.9 5.2 fusion.13
  81.7 7.0 %collective-permute-start.1 = (f32[32,512]{1,0:T(8,128)S(1)}, f32[32,512]{1,0:T(8,128)S(1)}, u32[]{:S(2)}, u32[]{:S(2)}) collective-permute-start(f32[32,512]{1,0:T(8,128)S(1)} %copy-done.55), channel_id=1, source_target_pairs={{0,2},{1,3},{2,4},{3,5},{4,6},{5,7},{6,8},{7,9},{8,10},{9,11},{10,... | collective-permute-start | bytes 196616 | tf_op jit(solution)/shard_map/ppermute | solution.py:17
  90.7 7.1 %collective-permute-start.2 = (f32[32,512]{1,0:T(8,128)S(1)}, f32[32,512]{1,0:T(8,128)S(1)}, u32[]{:S(2)}, u32[]{:S(2)}) collective-permute-start(f32[32,512]{1,0:T(8,128)S(1)} %copy-done.54), channel_id=1, source_target_pairs={{0,3},{1,4},{2,5},{3,6},{4,7},{5,8},{6,9},{7,10},{8,11},{9,12},{10... | collective-permute-start | bytes 196616 | tf_op jit(solution)/shard_map/ppermute | solution.py:17
  99.6 5.2 collective-permute-start.3
  114.0 50.2 %gather_fusion.4 = f32[4608,32]{1,0:T(8,128)} fusion(f32[288,16,32]{2,1,0:T(8,128)S(1)} %copy.303, s32[4608]{0:T(1024)S(1)} %reshape.372), kind=kCustom, calls=%fused_computation.clone | custom fusion | bytes 1216512 | tf_op jit(solution)/shard_map/jit(take_along_axis)/gather | solution.py:109
  190.8 8.4 %collective-permute-start.14 = (f32[32,512]{1,0:T(8,128)S(1)}, f32[32,512]{1,0:T(8,128)S(1)}, u32[]{:S(2)}, u32[]{:S(2)}) collective-permute-start(f32[32,512]{1,0:T(8,128)S(1)} %get-tuple-element.46), channel_id=1, source_target_pairs={{3,0},{4,1},{5,2},{6,3},{7,4},{8,5},{9,6},{10,7},{11,8},{12,9},{13... | collective-permute-start | bytes 196616 | tf_op jit(solution)/shard_map/ppermute | solution.py:17
  203.0 12.1 %collective-permute-start.9 = (f32[32,512]{1,0:T(8,128)S(1)}, f32[32,512]{1,0:T(8,128)S(1)}, u32[]{:S(2)}, u32[]{:S(2)}) collective-permute-start(f32[32,512]{1,0:T(8,128)S(1)} %get-tuple-element.51), channel_id=1, source_target_pairs={{0,2},{1,3},{2,4},{3,5},{4,6},{5,7},{6,8},{7,9},{8,10},{9,11},{10,... | collective-permute-start | bytes 196616 | tf_op jit(solution)/shard_map/ppermute | solution.py:17
  217.0 7.0 %collective-permute-start.10 = (f32[32,512]{1,0:T(8,128)S(1)}, f32[32,512]{1,0:T(8,128)S(1)}, u32[]{:S(2)}, u32[]{:S(2)}) collective-permute-start(f32[32,512]{1,0:T(8,128)S(1)} %get-tuple-element.50), channel_id=1, source_target_pairs={{0,3},{1,4},{2,5},{3,6},{4,7},{5,8},{6,9},{7,10},{8,11},{9,12},{10... | collective-permute-start | bytes 196616 | tf_op jit(solution)/shard_map/ppermute | solution.py:17
  225.9 6.6 %collective-permute-start.11 = (f32[32,512]{1,0:T(8,128)S(1)}, f32[32,512]{1,0:T(8,128)S(1)}, u32[]{:S(2)}, u32[]{:S(2)}) collective-permute-start(f32[32,512]{1,0:T(8,128)S(1)} %get-tuple-element.49), channel_id=1, source_target_pairs={{0,4},{1,5},{2,6},{3,7},{4,8},{5,9},{6,10},{7,11},{8,12},{9,13},{1... | collective-permute-start | bytes 196616 | tf_op jit(solution)/shard_map/ppermute | solution.py:17
  239.9 50.2 %gather_fusion.5 = f32[4608,32]{1,0:T(8,128)} fusion(f32[288,16,32]{2,1,0:T(8,128)S(1)} %copy.326, s32[4608]{0:T(1024)S(1)} %reshape.372), kind=kCustom, calls=%fused_computation.1.clone | custom fusion | bytes 1216512 | tf_op jit(solution)/shard_map/jit(take_along_axis)/gather | solution.py:109
  320.5 25.9 %scatter_custom_fusion.4 = f32[4608,32]{1,0:T(8,128)S(1)} fusion(s32[4608]{0:T(1024)} %reshape.352, f32[4608,32]{1,0:T(8,128)} %bitcast.356, f32[]{:T(128)} %constant.17.clone.1), kind=kCustom, calls=%fused_computation.56 | custom fusion | flops 147456 | bytes 590336
  350.2 8.8 %collective-permute-start.23 = (f32[32,512]{1,0:T(8,128)S(1)}, f32[32,512]{1,0:T(8,128)S(1)}, u32[]{:S(2)}, u32[]{:S(2)}) collective-permute-start(f32[32,512]{1,0:T(8,128)S(1)} %get-tuple-element.37), channel_id=1, source_target_pairs={{0,4},{1,5},{2,6},{3,7},{4,8},{5,9},{6,10},{7,11},{8,12},{9,13},{1... | collective-permute-start | bytes 196616 | tf_op jit(solution)/shard_map/ppermute | solution.py:17
  361.1 4.8 collective-permute-start.21
  376.1 7.6 %collective-permute-done.17 = f32[32,512]{1,0:T(8,128)S(1)} collective-permute-done((f32[32,512]{1,0:T(8,128)S(1)}, f32[32,512]{1,0:T(8,128)S(1)}, u32[]{:S(2)}, u32[]{:S(2)}) %collective-permute-start.17) | collective-permute-done | bytes 65568 | tf_op jit(solution)/shard_map/ppermute | solution.py:17
  385.7 8.2 %collective-permute-done.18 = f32[32,512]{1,0:T(8,128)S(1)} collective-permute-done((f32[32,512]{1,0:T(8,128)S(1)}, f32[32,512]{1,0:T(8,128)S(1)}, u32[]{:S(2)}, u32[]{:S(2)}) %collective-permute-start.18) | collective-permute-done | bytes 65568 | tf_op jit(solution)/shard_map/ppermute | solution.py:17
  395.8 8.7 %collective-permute-done.19 = f32[32,512]{1,0:T(8,128)S(1)} collective-permute-done((f32[32,512]{1,0:T(8,128)S(1)}, f32[32,512]{1,0:T(8,128)S(1)}, u32[]{:S(2)}, u32[]{:S(2)}) %collective-permute-start.19) | collective-permute-done | bytes 65568 | tf_op jit(solution)/shard_map/ppermute | solution.py:17
  452.1 5.3 fusion.4
  461.7 25.9 %scatter_custom_fusion.5 = f32[4608,32]{1,0:T(8,128)S(1)} fusion(s32[4608]{0:T(1024)} %reshape.352, f32[4608,32]{1,0:T(8,128)} %bitcast.355, f32[]{:T(128)} %constant.17.clone.1), kind=kCustom, calls=%fused_computation.54 | custom fusion | flops 147456 | bytes 590336
  506.7 68.0 %all-reduce.4 = (f32[1,64,64]{2,1,0:T(8,128)S(1)}, f32[1,64,64]{2,1,0:T(8,128)S(1)}, f32[1,64]{1,0:T(1,128)S(1)}, f32[1,64]{1,0:T(1,128)S(1)}, f32[1,64,32]{1,2,0:T(8,128)S(1)}, /*index=5*/f32[1,64,32]{1,2,0:T(8,128)S(1)}) all-reduce(f32[1,64,64]{2,1,0:T(8,128)S(1)} %copy-done.44, ...), channel_id=1, replica_groups=mesh['dom'=128] {'dom'}, use_global_device_ids=true, to_apply=%region_8.10 | all-reduce | flops 12416 | bytes 99328 | tf_op jit(solution)/shard_map/psum | solution.py:220
  579.4 7.5 %collective-permute-done.25 = f32[32,512]{1,0:T(8,128)S(1)} collective-permute-done((f32[32,512]{1,0:T(8,128)S(1)}, f32[32,512]{1,0:T(8,128)S(1)}, u32[]{:S(2)}, u32[]{:S(2)}) %collective-permute-start.25) | collective-permute-done | bytes 65568 | tf_op jit(solution)/shard_map/ppermute | solution.py:17
  588.9 7.9 %collective-permute-done.26 = f32[32,512]{1,0:T(8,128)S(1)} collective-permute-done((f32[32,512]{1,0:T(8,128)S(1)}, f32[32,512]{1,0:T(8,128)S(1)}, u32[]{:S(2)}, u32[]{:S(2)}) %collective-permute-start.26) | collective-permute-done | bytes 65568 | tf_op jit(solution)/shard_map/ppermute | solution.py:17
  598.7 8.7 %collective-permute-done.27 = f32[32,512]{1,0:T(8,128)S(1)} collective-permute-done((f32[32,512]{1,0:T(8,128)S(1)}, f32[32,512]{1,0:T(8,128)S(1)}, u32[]{:S(2)}, u32[]{:S(2)}) %collective-permute-start.27) | collective-permute-done | bytes 65568 | tf_op jit(solution)/shard_map/ppermute | solution.py:17
  610.7 4.7 convolution_bitcast_fusion.16
  (352 shorter events, 259.3 us)
Async XLA Ops:
  11.9 97.9 %collective-permute-start.7 = (f32[32,512]{1,0:T(8,128)}, f32[32,512]{1,0:T(8,128)}, u32[]{:S(2)}, u32[]{:S(2)}) collective-permute-start(f32[32,512]{1,0:T(8,128)} %get-tuple-element.53), channel_id=1, source_target_pairs={{4,0},{5,1},{6,2},{7,3},{8,4},{9,5},{10,6},{11,7},{12,8},{13,9},{1... | collective-permute-start | bytes 196616 | tf_op jit(solution)/shard_map/ppermute | solution.py:17
  15.0 94.0 %collective-permute-start.6 = (f32[32,512]{1,0:T(8,128)}, f32[32,512]{1,0:T(8,128)}, u32[]{:S(2)}, u32[]{:S(2)}) collective-permute-start(f32[32,512]{1,0:T(8,128)} %get-tuple-element.54), channel_id=1, source_target_pairs={{3,0},{4,1},{5,2},{6,3},{7,4},{8,5},{9,6},{10,7},{11,8},{12,9},{13... | collective-permute-start | bytes 196616 | tf_op jit(solution)/shard_map/ppermute | solution.py:17
  18.7 89.5 %collective-permute-start.5 = (f32[32,512]{1,0:T(8,128)}, f32[32,512]{1,0:T(8,128)}, u32[]{:S(2)}, u32[]{:S(2)}) collective-permute-start(f32[32,512]{1,0:T(8,128)} %get-tuple-element.55), channel_id=1, source_target_pairs={{2,0},{3,1},{4,2},{5,3},{6,4},{7,5},{8,6},{9,7},{10,8},{11,9},{12,... | collective-permute-start | bytes 196616 | tf_op jit(solution)/shard_map/ppermute | solution.py:17
  21.3 85.9 %collective-permute-start.4 = (f32[32,512]{1,0:T(8,128)}, f32[32,512]{1,0:T(8,128)}, u32[]{:S(2)}, u32[]{:S(2)}) collective-permute-start(f32[32,512]{1,0:T(8,128)} %get-tuple-element.56), channel_id=1, source_target_pairs={{1,0},{2,1},{3,2},{4,3},{5,4},{6,5},{7,6},{8,7},{9,8},{10,9},{11,1... | collective-permute-start | bytes 196616 | tf_op jit(solution)/shard_map/ppermute | solution.py:17
  24.1 57.6 %collective-permute-start = (f32[32,512]{1,0:T(8,128)}, f32[32,512]{1,0:T(8,128)}, u32[]{:S(2)}, u32[]{:S(2)}) collective-permute-start(f32[32,512]{1,0:T(8,128)} %get-tuple-element.60), channel_id=1, source_target_pairs={{0,1},{1,2},{2,3},{3,4},{4,5},{5,6},{6,7},{7,8},{8,9},{9,10},{10,1... | collective-permute-start | bytes 196616 | tf_op jit(solution)/shard_map/ppermute | solution.py:17
  184.3 18.7 %collective-permute-start.8 = (f32[32,512]{1,0:T(8,128)S(1)}, f32[32,512]{1,0:T(8,128)S(1)}, u32[]{:S(2)}, u32[]{:S(2)}) collective-permute-start(f32[32,512]{1,0:T(8,128)S(1)} %get-tuple-element.52), channel_id=1, source_target_pairs={{0,1},{1,2},{2,3},{3,4},{4,5},{5,6},{6,7},{7,8},{8,9},{9,10},{10,1... | collective-permute-start | bytes 196616 | tf_op jit(solution)/shard_map/ppermute | solution.py:17
  188.4 46.1 %collective-permute-start.15 = (f32[32,512]{1,0:T(8,128)S(1)}, f32[32,512]{1,0:T(8,128)S(1)}, u32[]{:S(2)}, u32[]{:S(2)}) collective-permute-start(f32[32,512]{1,0:T(8,128)S(1)} %get-tuple-element.45), channel_id=1, source_target_pairs={{4,0},{5,1},{6,2},{7,3},{8,4},{9,5},{10,6},{11,7},{12,8},{13,9},{1... | collective-permute-start | bytes 196616 | tf_op jit(solution)/shard_map/ppermute | solution.py:17
  190.8 43.7 %collective-permute-start.14 = (f32[32,512]{1,0:T(8,128)S(1)}, f32[32,512]{1,0:T(8,128)S(1)}, u32[]{:S(2)}, u32[]{:S(2)}) collective-permute-start(f32[32,512]{1,0:T(8,128)S(1)} %get-tuple-element.46), channel_id=1, source_target_pairs={{3,0},{4,1},{5,2},{6,3},{7,4},{8,5},{9,6},{10,7},{11,8},{12,9},{13... | collective-permute-start | bytes 196616 | tf_op jit(solution)/shard_map/ppermute | solution.py:17
  199.2 35.3 %collective-permute-start.13 = (f32[32,512]{1,0:T(8,128)S(1)}, f32[32,512]{1,0:T(8,128)S(1)}, u32[]{:S(2)}, u32[]{:S(2)}) collective-permute-start(f32[32,512]{1,0:T(8,128)S(1)} %get-tuple-element.47), channel_id=1, source_target_pairs={{2,0},{3,1},{4,2},{5,3},{6,4},{7,5},{8,6},{9,7},{10,8},{11,9},{12,... | collective-permute-start | bytes 196616 | tf_op jit(solution)/shard_map/ppermute | solution.py:17
  201.1 33.3 %collective-permute-start.12 = (f32[32,512]{1,0:T(8,128)S(1)}, f32[32,512]{1,0:T(8,128)S(1)}, u32[]{:S(2)}, u32[]{:S(2)}) collective-permute-start(f32[32,512]{1,0:T(8,128)S(1)} %get-tuple-element.48), channel_id=1, source_target_pairs={{1,0},{2,1},{3,2},{4,3},{5,4},{6,5},{7,6},{8,7},{9,8},{10,9},{11,1... | collective-permute-start | bytes 196616 | tf_op jit(solution)/shard_map/ppermute | solution.py:17
  203.0 14.0 %collective-permute-start.9 = (f32[32,512]{1,0:T(8,128)S(1)}, f32[32,512]{1,0:T(8,128)S(1)}, u32[]{:S(2)}, u32[]{:S(2)}) collective-permute-start(f32[32,512]{1,0:T(8,128)S(1)} %get-tuple-element.51), channel_id=1, source_target_pairs={{0,2},{1,3},{2,4},{3,5},{4,6},{5,7},{6,8},{7,9},{8,10},{9,11},{10,... | collective-permute-start | bytes 196616 | tf_op jit(solution)/shard_map/ppermute | solution.py:17
  350.2 54.4 %collective-permute-start.23 = (f32[32,512]{1,0:T(8,128)S(1)}, f32[32,512]{1,0:T(8,128)S(1)}, u32[]{:S(2)}, u32[]{:S(2)}) collective-permute-start(f32[32,512]{1,0:T(8,128)S(1)} %get-tuple-element.37), channel_id=1, source_target_pairs={{0,4},{1,5},{2,6},{3,7},{4,8},{5,9},{6,10},{7,11},{8,12},{9,13},{1... | collective-permute-start | bytes 196616 | tf_op jit(solution)/shard_map/ppermute | solution.py:17
  359.0 45.5 %collective-permute-start.22 = (f32[32,512]{1,0:T(8,128)S(1)}, f32[32,512]{1,0:T(8,128)S(1)}, u32[]{:S(2)}, u32[]{:S(2)}) collective-permute-start(f32[32,512]{1,0:T(8,128)S(1)} %get-tuple-element.38), channel_id=1, source_target_pairs={{0,3},{1,4},{2,5},{3,6},{4,7},{5,8},{6,9},{7,10},{8,11},{9,12},{10... | collective-permute-start | bytes 196616 | tf_op jit(solution)/shard_map/ppermute | solution.py:17
  361.1 43.4 %collective-permute-start.21 = (f32[32,512]{1,0:T(8,128)S(1)}, f32[32,512]{1,0:T(8,128)S(1)}, u32[]{:S(2)}, u32[]{:S(2)}) collective-permute-start(f32[32,512]{1,0:T(8,128)S(1)} %get-tuple-element.39), channel_id=1, source_target_pairs={{0,2},{1,3},{2,4},{3,5},{4,6},{5,7},{6,8},{7,9},{8,10},{9,11},{10,... | collective-permute-start | bytes 196616 | tf_op jit(solution)/shard_map/ppermute | solution.py:17
  365.9 38.6 %collective-permute-start.20 = (f32[32,512]{1,0:T(8,128)S(1)}, f32[32,512]{1,0:T(8,128)S(1)}, u32[]{:S(2)}, u32[]{:S(2)}) collective-permute-start(f32[32,512]{1,0:T(8,128)S(1)} %get-tuple-element.40), channel_id=1, source_target_pairs={{0,1},{1,2},{2,3},{3,4},{4,5},{5,6},{6,7},{7,8},{8,9},{9,10},{10,1... | collective-permute-start | bytes 196616 | tf_op jit(solution)/shard_map/ppermute | solution.py:17
  373.4 10.4 %collective-permute-start.17 = (f32[32,512]{1,0:T(8,128)S(1)}, f32[32,512]{1,0:T(8,128)S(1)}, u32[]{:S(2)}, u32[]{:S(2)}) collective-permute-start(f32[32,512]{1,0:T(8,128)S(1)} %get-tuple-element.43), channel_id=1, source_target_pairs={{2,0},{3,1},{4,2},{5,3},{6,4},{7,5},{8,6},{9,7},{10,8},{11,9},{12,... | collective-permute-start | bytes 196616 | tf_op jit(solution)/shard_map/ppermute | solution.py:17
  393.8 10.7 %collective-permute-start.19 = (f32[32,512]{1,0:T(8,128)S(1)}, f32[32,512]{1,0:T(8,128)S(1)}, u32[]{:S(2)}, u32[]{:S(2)}) collective-permute-start(f32[32,512]{1,0:T(8,128)S(1)} %get-tuple-element.41), channel_id=1, source_target_pairs={{4,0},{5,1},{6,2},{7,3},{8,4},{9,5},{10,6},{11,7},{12,8},{13,9},{1... | collective-permute-start | bytes 196616 | tf_op jit(solution)/shard_map/ppermute | solution.py:17
  491.5 115.9 %collective-permute-start.31 = (f32[32,512]{1,0:T(8,128)S(1)}, f32[32,512]{1,0:T(8,128)S(1)}, u32[]{:S(2)}, u32[]{:S(2)}) collective-permute-start(f32[32,512]{1,0:T(8,128)S(1)} %get-tuple-element.29), channel_id=1, source_target_pairs={{0,4},{1,5},{2,6},{3,7},{4,8},{5,9},{6,10},{7,11},{8,12},{9,13},{1... | collective-permute-start | bytes 196616 | tf_op jit(solution)/shard_map/ppermute | solution.py:17
  495.1 112.4 %collective-permute-start.30 = (f32[32,512]{1,0:T(8,128)S(1)}, f32[32,512]{1,0:T(8,128)S(1)}, u32[]{:S(2)}, u32[]{:S(2)}) collective-permute-start(f32[32,512]{1,0:T(8,128)S(1)} %get-tuple-element.30), channel_id=1, source_target_pairs={{0,3},{1,4},{2,5},{3,6},{4,7},{5,8},{6,9},{7,10},{8,11},{9,12},{10... | collective-permute-start | bytes 196616 | tf_op jit(solution)/shard_map/ppermute | solution.py:17
  497.0 110.4 %collective-permute-start.29 = (f32[32,512]{1,0:T(8,128)S(1)}, f32[32,512]{1,0:T(8,128)S(1)}, u32[]{:S(2)}, u32[]{:S(2)}) collective-permute-start(f32[32,512]{1,0:T(8,128)S(1)} %get-tuple-element.31), channel_id=1, source_target_pairs={{0,2},{1,3},{2,4},{3,5},{4,6},{5,7},{6,8},{7,9},{8,10},{9,11},{10,... | collective-permute-start | bytes 196616 | tf_op jit(solution)/shard_map/ppermute | solution.py:17
  501.0 106.4 %collective-permute-start.28 = (f32[32,512]{1,0:T(8,128)S(1)}, f32[32,512]{1,0:T(8,128)S(1)}, u32[]{:S(2)}, u32[]{:S(2)}) collective-permute-start(f32[32,512]{1,0:T(8,128)S(1)} %get-tuple-element.32), channel_id=1, source_target_pairs={{0,1},{1,2},{2,3},{3,4},{4,5},{5,6},{6,7},{7,8},{8,9},{9,10},{10,1... | collective-permute-start | bytes 196616 | tf_op jit(solution)/shard_map/ppermute | solution.py:17
  503.0 73.6 %collective-permute-start.24 = (f32[32,512]{1,0:T(8,128)S(1)}, f32[32,512]{1,0:T(8,128)S(1)}, u32[]{:S(2)}, u32[]{:S(2)}) collective-permute-start(f32[32,512]{1,0:T(8,128)S(1)} %get-tuple-element.36), channel_id=1, source_target_pairs={{1,0},{2,1},{3,2},{4,3},{5,4},{6,5},{7,6},{8,7},{9,8},{10,9},{11,1... | collective-permute-start | bytes 196616 | tf_op jit(solution)/shard_map/ppermute | solution.py:17
  576.6 10.4 %collective-permute-start.25 = (f32[32,512]{1,0:T(8,128)S(1)}, f32[32,512]{1,0:T(8,128)S(1)}, u32[]{:S(2)}, u32[]{:S(2)}) collective-permute-start(f32[32,512]{1,0:T(8,128)S(1)} %get-tuple-element.35), channel_id=1, source_target_pairs={{2,0},{3,1},{4,2},{5,3},{6,4},{7,5},{8,6},{9,7},{10,8},{11,9},{12,... | collective-permute-start | bytes 196616 | tf_op jit(solution)/shard_map/ppermute | solution.py:17
  596.7 10.7 %collective-permute-start.27 = (f32[32,512]{1,0:T(8,128)S(1)}, f32[32,512]{1,0:T(8,128)S(1)}, u32[]{:S(2)}, u32[]{:S(2)}) collective-permute-start(f32[32,512]{1,0:T(8,128)S(1)} %get-tuple-element.33), channel_id=1, source_target_pairs={{4,0},{5,1},{6,2},{7,3},{8,4},{9,5},{10,6},{11,7},{12,8},{13,9},{1... | collective-permute-start | bytes 196616 | tf_op jit(solution)/shard_map/ppermute | solution.py:17
  (76 other events, 600.1 us)
where the time goes:
time: 625 us; the launch traced here: 619 us
  local copies, waits for them, and re-layouts  164 us (26%)
  starting transfers between devices  125 us (20%)
  matrix products  120 us (19%)
  other arithmetic  77.5 us (12%)
  blocking collectives  68 us (11%)
  waiting for transfers between devices  60.8 us (10%)
    ppermute x32, starting transfers between devices, shifted(): lax.ppermute(value, axis, [(source, source + steps) for source in range(i...  125 us
    gather x4, local copies, waits for them, and re-layouts, outer_traces(): turned = jnp.take_along_axis(tiles, orient_rows[:, :, None], axis=1)  101 us
    psum x1, blocking collectives, local(): summed[layer] = lax.psum((grad_one, grad_bias, grad_two), 'dom')  68 us
    ppermute x32, waiting for transfers between devices, shifted(): lax.ppermute(value, axis, [(source, source + steps) for source in range(i...  60.8 us
    unnamed x5, other arithmetic  52 us
    dot_general x6, matrix products, flux_step(): jnp.dot(outer_rows, weight_one[width:], precision=HIGHEST)  24.1 us
    dot_general x6, matrix products, flux_step(): jnp.dot(inner_rows, weight_one[:width], precision=HIGHEST)  17.8 us
    dot_general x3, matrix products, flux_step(): along_k = jnp.einsum('ak,eijkc->eijac', deriv, cube, precision=HIGHEST)  12.7 us
  transfers between devices with their start and end apart: 32, of which 13 were waited for; matrix products, arithmetic and copies ran while one was open for 10% of the time, Pallas kernels for 0%

commit v1 on v0

v1 whole, which is shorter than its diff:
```python
import functools

import jax
import jax.numpy as jnp
import numpy as np
from jax import lax
from jax.experimental import pallas as pl
from jax.experimental.pallas import tpu as pltpu
from jax.sharding import PartitionSpec as P

MESH = pl.DeviceIdType.MESH
HIGHEST = lax.Precision.HIGHEST
F32 = jnp.float32
BF16 = jnp.bfloat16
I32 = jnp.int32
NEIGH = 4
BLOCKS = 2 * NEIGH
CAP = 32
SLOTS = BLOCKS * CAP
STEP_SIZE = 0.25
E = 48
FACES = 6 * E
OFFSETS = [level + 1 for level in range(NEIGH)] + [-(level + 1) for level in range(NEIGH)]


def deriv_matrix():
    points = np.array([-1.0, -np.sqrt(0.2), np.sqrt(0.2), 1.0])
    weights = np.array(
        [np.prod([points[r] - points[o] for o in range(4) if o != r]) for r in range(4)]
    )
    matrix = np.zeros((4, 4))
    for r in range(4):
        for c in range(4):
            if r != c:
                matrix[r, c] = weights[r] / weights[c] / (points[r] - points[c])
        matrix[r, r] = -np.sum(matrix[r])
    return matrix


DERIV = deriv_matrix()


def iota(shape, dim):
    return lax.broadcasted_iota(I32, shape, dim)


def dot(a, b):
    return jnp.dot(a, b, preferred_element_type=F32)


def dot_nt(a, b):
    return lax.dot_general(a, b, (((1,), (1,)), ((), ())), preferred_element_type=F32)


def dot_tn(a, b):
    return lax.dot_general(a, b, (((0,), (0,)), ((), ())), preferred_element_type=F32)


def dot_full(a, b):
    return jnp.dot(a, b, preferred_element_type=F32, precision=HIGHEST)


def split(x):
    high = x.astype(BF16)
    return high, (x - high.astype(F32)).astype(BF16)


def three(op, a, b):
    return op(a[0], b[0]) + op(a[1], b[0]) + op(a[0], b[1])


def lanes(a):
    return pl.ds(pl.multiple_of(a * 128, 128), 128)


def ones_where(match, dtype=F32):
    return jnp.where(match, 1.0, 0.0).astype(dtype)


def kernel(
    count,
    state_ref, cot_ref, live_ref, src_ref, orient_ref, send_ref, vol_ref, w1_ref, b1_ref, w2_ref, deriv_ref,
    out_ref, out_w1, out_b1, out_w2,
    field, grad, volume, vol_y, vol_xh, vol_xl,
    trace_h, trace_l, raw, pair_h, pair_l, hid, flux, gflux_h, gflux_l, gpre_h, gpre_l, gin, gout, turn_h, turn_l,
    sel, sel_t, loc, rem, loc_t, rem_t, masks,
    w1h, w1l, w2h, w2l, vh, vl, vth, vtl, bias,
    sent, got, packed, part, part_sum, total,
    send_sem, recv_sem, ar_send, ar_recv,
):
    me = lax.axis_index("dom")
    group = 16
    others = count // group
    base = (me // group) * group
    mine = lax.rem(me, group)
    rank = me // group

    def neighbour(offset):
        return lax.rem(me + offset + count, count)

    def in_group(step):
        return base + lax.rem(mine + step, group)

    def across(step):
        return lax.rem(rank + step, others) * group + mine

    barrier = pltpu.get_barrier_semaphore()
    partners = [neighbour(o) for o in OFFSETS]
    partners += [in_group(s) for s in range(1, group)]
    partners += [across(s) for s in range(1, others)]
    for device in partners:
        pl.semaphore_signal(barrier, inc=1, device_id=(device,), device_id_type=MESH)

    def exchange(which, sign):
        copies = []
        for block in (3, 7, 2, 6, 1, 5, 0, 4):
            rows = pl.ds(block * CAP, CAP)
            copies.append(
                pltpu.make_async_remote_copy(
                    src_ref=sent.at[which, rows],
                    dst_ref=got.at[which, rows],
                    send_sem=send_sem.at[which, block],
                    recv_sem=recv_sem.at[which, block],
                    device_id=(neighbour(sign * OFFSETS[block]),),
                    device_id_type=MESH,
                )
            )
        for copy in copies:
            copy.start()
        return copies

    for f in range(6):
        sel_t[f * E : (f + 1) * E, :] = ones_where(6 * iota((E, SLOTS), 0) + f == send_ref[...], BF16)
    eye = ones_where(iota((SLOTS, SLOTS), 0) == iota((SLOTS, SLOTS), 1), BF16)
    sel[...] = dot_nt(eye, sel_t[...]).astype(BF16)

    def tile(ref, n):
        return ref[:, n * 128 : (n + 1) * 128]

    group_of_lane = iota((E, 128), 1) >> 5

    def traces(ref, emit):
        for a in range(4):
            emit(0, a, tile(ref, a))
            emit(1, a, tile(ref, 12 + a))
            emit(2, a, tile(ref, 4 * a))
            emit(3, a, tile(ref, 4 * a + 3))
            first = tile(ref, 4 * a)
            last = pltpu.roll(tile(ref, 4 * a), 32, 1)
            for b in range(1, 4):
                node = tile(ref, 4 * a + b)
                first = jnp.where(group_of_lane == b, pltpu.roll(node, 32 * b, 1), first)
                moved = node if b == 3 else pltpu.roll(node, 32 * (b + 1), 1)
                last = jnp.where(group_of_lane == b, moved, last)
            emit(4, a, first)
            emit(5, a, last)

    def lift(ref, i, j):
        at = lambda f, a: ref[f * E : (f + 1) * E, a * 128 : (a + 1) * 128]
        low, high = at(4, i), at(5, i)
        low = pltpu.roll(low, (128 - 32 * j) % 128, 1) if j else low
        high = pltpu.roll(high, 96 - 32 * j, 1) if j < 3 else high
        value = jnp.where(group_of_lane == 0, low, jnp.where(group_of_lane == 3, high, 0.0))
        if i == 0:
            value = value + at(0, j)
        if i == 3:
            value = value + at(1, j)
        if j == 0:
            value = value + at(2, i)
        if j == 3:
            value = value + at(3, i)
        return value

    def keep_traces(layer):
        def emit(f, a, value):
            high, low = split(value)
            rows, cols = slice(f * E, (f + 1) * E), slice(a * 128, (a + 1) * 128)
            trace_h[rows, cols] = high
            trace_l[rows, cols] = low
            pair_h[layer, a, rows, 0:128] = high
            pair_l[layer, a, rows, 0:128] = low

        return emit

    def keep_gflux(f, a, value):
        high, low = split(STEP_SIZE * value)
        rows, cols = slice(f * E, (f + 1) * E), slice(a * 128, (a + 1) * 128)
        gflux_h[rows, cols] = high
        gflux_l[rows, cols] = low

    def volume_of(ref, layer, adjoint):
        for n in range(16):
            high, low = split(tile(ref, n))
            vol_xh[n * E : (n + 1) * E, :] = high
            vol_xl[n * E : (n + 1) * E, :] = low
        wh, wl = (vth, vtl) if adjoint else (vh, vl)
        vol_y[...] = three(dot, (vol_xh[...], vol_xl[...]), (wh[layer], wl[layer]))
        deriv = DERIV.T if adjoint else DERIV
        for i in range(4):
            for j in range(4):
                n = 4 * i + j
                value = vol_y[n * E : (n + 1) * E, 256:384]
                for o in range(4):
                    if abs(deriv[i, o]) > 1e-12:
                        at = 4 * o + j
                        value = value + float(deriv[i, o]) * vol_y[at * E : (at + 1) * E, 0:128]
                    if abs(deriv[j, o]) > 1e-12:
                        at = 4 * i + o
                        value = value + float(deriv[j, o]) * vol_y[at * E : (at + 1) * E, 128:256]
                volume[:, n * 128 : (n + 1) * 128] = value

    def flip_lanes(x, even):
        return jnp.where(even, pltpu.roll(x, 32, 1), pltpu.roll(x, 96, 1))

    def swap(x, by_group):
        odd, upper = by_group
        stage = [None] * 4
        for a in (0, 2):
            stage[a] = jnp.where(odd, pltpu.roll(x[a + 1], 32, 1), x[a])
            stage[a + 1] = jnp.where(odd, x[a + 1], pltpu.roll(x[a], 96, 1))
        out = [None] * 4
        for a in (0, 1):
            out[a] = jnp.where(upper, pltpu.roll(stage[a + 2], 64, 1), stage[a])
            out[a + 2] = jnp.where(upper, stage[a + 2], pltpu.roll(stage[a], 64, 1))
        return out

    def lane_masks():
        groups = iota((E, 128), 1) >> 5
        return (groups & 1) == 1, groups >= 2

    def row_masks(rows):
        return [masks[rows, m * 128 : (m + 1) * 128] > 0.5 for m in range(3)]

    def orient_rows(layer):
        def body(step, carry):
            rows = pl.ds(pl.multiple_of(step * E, E), E)
            odd, upper = lane_masks()
            up, across_, turned = row_masks(rows)
            x = [raw[rows, a * 128 : (a + 1) * 128] for a in range(4)]
            x = [jnp.where(up, x[3 - a], x[a]) for a in range(4)]
            x = [jnp.where(across_, flip_lanes(v, jnp.logical_not(odd)), v) for v in x]
            y = swap(x, (odd, upper))
            for a in range(4):
                high, low = split(jnp.where(turned, y[a], x[a]))
                pair_h[layer, a, rows, 128:256] = high
                pair_l[layer, a, rows, 128:256] = low
            return carry

        lax.fori_loop(0, 6, body, 0)

    def turn_back_rows():
        def body(step, carry):
            rows = pl.ds(pl.multiple_of(step * E, E), E)
            odd, upper = lane_masks()
            up, across_, turned = row_masks(rows)
            x = [gout[rows, a * 128 : (a + 1) * 128] for a in range(4)]
            y = swap(x, (odd, upper))
            x = [jnp.where(turned, y[a], x[a]) for a in range(4)]
            x = [jnp.where(across_, flip_lanes(v, jnp.logical_not(odd)), v) for v in x]
            for a in range(4):
                high, low = split(jnp.where(up, x[3 - a], x[a]))
                turn_h[rows, a * 128 : (a + 1) * 128] = high
                turn_l[rows, a * 128 : (a + 1) * 128] = low
            return carry

        lax.fori_loop(0, 6, body, 0)

    def hidden_of(layer, with_flux):
        def body(a, carry):
            x = (pair_h[layer, a], pair_l[layer, a])
            h = jnp.tanh(three(dot, x, (w1h[layer], w1l[layer])) + bias[layer, 0:1, :])
            hid[layer, a] = h
            if with_flux:
                flux[:, lanes(a)] = three(dot, split(h), (w2h[layer], w2l[layer]))
            return carry

        lax.fori_loop(0, 4, body, 0)

    def flux_back(layer):
        def body(a, carry):
            g = (gflux_h[:, lanes(a)], gflux_l[:, lanes(a)])
            h = hid[layer, a]
            pre = split(three(dot_nt, g, (w2h[layer], w2l[layer])) * (1.0 - h * h))
            gpre_h[a] = pre[0]
            gpre_l[a] = pre[1]
            both = three(dot_nt, pre, (w1h[layer], w1l[layer]))
            gin[:, lanes(a)] = both[:, 0:128]
            gout[:, lanes(a)] = both[:, 128:256]
            return carry

        lax.fori_loop(0, 4, body, 0)

    def weight_grads(layer):
        def body(a, carry):
            one, two, row = carry
            x = (pair_h[layer, a], pair_l[layer, a])
            pre = (gpre_h[a], gpre_l[a])
            g = (gflux_h[:, lanes(a)], gflux_l[:, lanes(a)])
            one = one + three(dot_tn, x, pre)
            two = two + three(dot_tn, split(hid[layer, a]), g)
            row = row + jnp.sum(pre[0].astype(F32) + pre[1].astype(F32), axis=0, keepdims=True)
            return one, two, row

        zeros = lambda *shape: jnp.zeros(shape, F32)
        one, two, row = lax.fori_loop(0, 4, body, (zeros(256, 256), zeros(256, 128), zeros(1, 256)))
        r, c = iota((256, 256), 0), iota((256, 256), 1)
        one = jnp.where(((r >> 5) & 3) == (c >> 6), one, 0.0)
        r, c = iota((256, 128), 0), iota((256, 128), 1)
        two = jnp.where((r >> 6) == (c >> 5), two, 0.0)
        r, c = iota((64, 256), 0), iota((64, 256), 1)
        pick_in = ones_where(r == ((c >> 7) * 32 + (c & 31)))
        pick_hid = ones_where(r == (c & 63))
        r, c = iota((256, 128), 0), iota((256, 128), 1)
        place_one = ones_where((r & 63) == c)
        place_bias = ones_where(c == 96)
        r, c = iota((128, 128), 0), iota((128, 128), 1)
        place_two = ones_where((r & 31) + 64 == c)
        value = dot_full(pick_in, dot_full(one, place_one))
        value = value + dot_full(pick_hid, dot_full(two, place_two))
        value = value + dot_full(pick_hid * row, place_bias)
        packed[layer * 64 : (layer + 1) * 64, :] = value

    alive = iota((E, 128), 0) < live_ref[0]
    for n in range(16):
        field[:, n * 128 : (n + 1) * 128] = jnp.where(alive, tile(state_ref, n), 0.0)
    traces(field, keep_traces(0))
    sent[0] = dot(sel[...], trace_h[...]) + dot(sel[...], trace_l[...])
    pl.semaphore_wait(barrier, len(partners))
    copies = exchange(0, 1)

    for f in range(6):
        rows = slice(f * E, (f + 1) * E)
        raw[rows, 0:FACES] = ones_where(6 * iota((E, FACES), 0) + f == iota((E, FACES), 1))
    order = raw[:, 0:FACES].astype(BF16)
    near = jnp.concatenate(
        [ones_where(6 * iota((E, FACES), 0) + f == src_ref[...], BF16) for f in range(6)], axis=0
    )
    far = ones_where(iota((SLOTS, FACES), 0) + FACES == src_ref[...], BF16)
    loc_t[...] = dot_nt(near, order).astype(BF16)
    loc[...] = dot_nt(order, near).astype(BF16)
    rem_t[...] = dot_nt(far, order).astype(BF16)
    rem[...] = dot_nt(order, far).astype(BF16)
    turn = orient_ref[...]
    flags = [(turn >> 1) & 1, (turn ^ (turn >> 1)) & 1, (turn ^ (turn >> 2)) & 1]
    for m in range(3):
        spread = jnp.broadcast_to(flags[m], (128, FACES)).astype(F32).astype(BF16)
        masks[:, m * 128 : (m + 1) * 128] = dot_nt(order, spread)

    for layer in range(2):
        r, c = iota((256, 64), 0), iota((256, 64), 1)
        rows_in = ones_where(c == ((r >> 7) * 32 + (r & 31)))
        rows_hid = ones_where(c == (r & 63))
        r, c = iota((64, 256), 0), iota((64, 256), 1)
        cols_hid = ones_where(r == (c & 63))
        r, c = iota((32, 128), 0), iota((32, 128), 1)
        cols_ch = ones_where(r == (c & 31))
        r, c = iota((128, 32), 0), iota((128, 32), 1)
        rows_ch = ones_where(c == (r & 31))
        r, c = iota((256, 256), 0), iota((256, 256), 1)
        big = dot_full(dot_full(rows_in, w1_ref[layer]), cols_hid)
        w1h[layer], w1l[layer] = split(jnp.where(((r >> 5) & 3) == (c >> 6), big, 0.0))
        r, c = iota((256, 128), 0), iota((256, 128), 1)
        big = dot_full(dot_full(rows_hid, w2_ref[layer]), cols_ch)
        w2h[layer], w2l[layer] = split(jnp.where((r >> 6) == (c >> 5), big, 0.0))
        r, c = iota((128, 128), 0), iota((128, 128), 1)
        same = (r >> 5) == (c >> 5)
        for axis in range(3):
            big = dot_full(dot_full(rows_ch, vol_ref[layer, axis]), cols_ch)
            big = jnp.where(same, big, 0.0) if axis < 2 else big * deriv_ref[...]
            cols = slice(axis * 128, (axis + 1) * 128)
            vh[layer, :, cols], vl[layer, :, cols] = split(big)
            vth[layer, :, cols], vtl[layer, :, cols] = split(big.T)
        bias[layer] = dot_full(jnp.broadcast_to(b1_ref[layer : layer + 1, :], (8, 64)), cols_hid)

    def gather_near():
        raw[...] = dot(loc[...], trace_h[...]) + dot(loc[...], trace_l[...])

    def gather_far(which):
        high, low = split(got[which])
        raw[...] += dot(rem[...], high) + dot(rem[...], low)

    gather_near()
    volume_of(field, 0, False)
    for copy in copies:
        copy.wait()
    gather_far(0)
    orient_rows(0)
    hidden_of(0, True)
    for n in range(16):
        cols = slice(n * 128, (n + 1) * 128)
        field[:, cols] += STEP_SIZE * (lift(flux, n // 4, n % 4) - volume[:, cols])

    traces(field, keep_traces(1))
    sent[1] = dot(sel[...], trace_h[...]) + dot(sel[...], trace_l[...])
    copies = exchange(1, 1)
    gather_near()
    traces(cot_ref, keep_gflux)
    volume_of(cot_ref, 1, True)
    for copy in copies:
        copy.wait()
    gather_far(1)
    orient_rows(1)
    hidden_of(1, False)

    def backward(layer, which, beside):
        flux_back(layer)
        turn_back_rows()
        sent[which] = dot(rem_t[...], turn_h[...]) + dot(rem_t[...], turn_l[...])
        copies = exchange(which, -1)
        gin[...] += dot(loc_t[...], turn_h[...]) + dot(loc_t[...], turn_l[...])
        beside()
        for copy in copies:
            copy.wait()
        high, low = split(got[which])
        gin[...] += dot(sel_t[...], high) + dot(sel_t[...], low)

    backward(1, 2, lambda: weight_grads(1))
    for n in range(16):
        cols = slice(n * 128, (n + 1) * 128)
        grad[:, cols] = tile(cot_ref, n) - STEP_SIZE * volume[:, cols] + lift(gin, n // 4, n % 4)
    traces(grad, keep_gflux)

    def reduce_grads():
        weight_grads(0)
        chunk = lambda j: pl.ds(pl.multiple_of(j * 8, 8), 8)
        stage = []
        for s in range(1, group):
            stage.append(
                pltpu.make_async_remote_copy(
                    src_ref=packed.at[chunk(lax.rem(mine + s, group))],
                    dst_ref=part.at[mine],
                    send_sem=ar_send.at[0, s],
                    recv_sem=ar_recv.at[0, s],
                    device_id=(in_group(s),),
                    device_id_type=MESH,
                )
            )
        for copy in stage:
            copy.start()
        part[mine] = packed[chunk(mine), :]
        volume_of(grad, 0, True)
        for copy in stage:
            copy.wait()
        value = part[0]
        for s in range(1, group):
            value = value + part[s]
        part_sum[rank] = value
        stage = []
        for s in range(1, others):
            stage.append(
                pltpu.make_async_remote_copy(
                    src_ref=part_sum.at[rank],
                    dst_ref=part_sum.at[rank],
                    send_sem=ar_send.at[1, s],
                    recv_sem=ar_recv.at[1, s],
                    device_id=(across(s),),
                    device_id_type=MESH,
                )
            )
        for copy in stage:
            copy.start()
        for copy in stage:
            copy.wait()
        value = part_sum[0]
        for s in range(1, others):
            value = value + part_sum[s]
        total[chunk(mine), :] = value
        stage = []
        for s in range(1, group):
            stage.append(
                pltpu.make_async_remote_copy(
                    src_ref=total.at[chunk(mine)],
                    dst_ref=total.at[chunk(mine)],
                    send_sem=ar_send.at[2, s],
                    recv_sem=ar_recv.at[2, s],
                    device_id=(in_group(s),),
                    device_id_type=MESH,
                )
            )
        for copy in stage:
            copy.start()
        for copy in stage:
            copy.wait()

    backward(0, 3, reduce_grads)
    for n in range(16):
        cols = slice(n * 128, (n + 1) * 128)
        value = grad[:, cols] - STEP_SIZE * volume[:, cols] + lift(gin, n // 4, n % 4)
        out_ref[:, cols] = jnp.where(alive, value, 0.0)
    factor = (2.0 * FACES * 8 * count) ** -0.5
    for layer in range(2):
        value = total[layer * 64 : (layer + 1) * 64, :] * factor
        out_w1[layer] = value[:, 0:64]
        out_w2[layer] = pltpu.roll(value, 64, 1)[:, 0:32]
        column = pltpu.roll(value, 32, 1)[:, 0:1]
        square = iota((64, 64), 0) == iota((64, 64), 1)
        out_b1[layer : layer + 1, :] = jnp.sum(jnp.where(square, column, 0.0), axis=0, keepdims=True)


def local(count, state, cotangent, elem_count, face_src, face_orient, send_face, vol_weight, w1, b1, w2):
    constant = np.zeros((128, 128), np.float32)
    for a in range(4):
        for k in range(4):
            constant[32 * k : 32 * k + 32, 32 * a : 32 * a + 32] = DERIV[a, k]
    vmem = pl.BlockSpec(memory_space=pltpu.VMEM)
    smem = pl.BlockSpec(memory_space=pltpu.SMEM)
    V = pltpu.VMEM
    scratch = [
        V((E, 2048), F32), V((E, 2048), F32), V((E, 2048), F32),
        V((16 * E, 384), F32), V((16 * E, 128), BF16), V((16 * E, 128), BF16),
        V((FACES, 512), BF16), V((FACES, 512), BF16), V((FACES, 512), F32),
        V((2, 4, FACES, 256), BF16), V((2, 4, FACES, 256), BF16), V((2, 4, FACES, 256), F32),
        V((FACES, 512), F32), V((FACES, 512), BF16), V((FACES, 512), BF16),
        V((4, FACES, 256), BF16), V((4, FACES, 256), BF16),
        V((FACES, 512), F32), V((FACES, 512), F32), V((FACES, 512), BF16), V((FACES, 512), BF16),
        V((SLOTS, FACES), BF16), V((FACES, SLOTS), BF16),
        V((FACES, FACES), BF16), V((FACES, SLOTS), BF16), V((FACES, FACES), BF16), V((SLOTS, FACES), BF16),
        V((FACES, 384), F32),
        V((2, 256, 256), BF16), V((2, 256, 256), BF16), V((2, 256, 128), BF16), V((2, 256, 128), BF16),
        V((2, 128, 384), BF16), V((2, 128, 384), BF16), V((2, 128, 384), BF16), V((2, 128, 384), BF16),
        V((2, 8, 256), F32),
        V((4, SLOTS, 512), F32), V((4, SLOTS, 512), F32),
        V((128, 128), F32), V((16, 8, 128), F32), V((count // 16, 8, 128), F32), V((128, 128), F32),
        pltpu.SemaphoreType.DMA((4, BLOCKS)), pltpu.SemaphoreType.DMA((4, BLOCKS)),
        pltpu.SemaphoreType.DMA((3, 16)), pltpu.SemaphoreType.DMA((3, 16)),
    ]
    return pl.pallas_call(
        functools.partial(kernel, count),
        out_shape=(
            jax.ShapeDtypeStruct(state.shape, F32),
            jax.ShapeDtypeStruct(w1.shape, F32),
            jax.ShapeDtypeStruct(b1.shape, F32),
            jax.ShapeDtypeStruct(w2.shape, F32),
        ),
        in_specs=[vmem, vmem, smem] + [vmem] * 8,
        out_specs=[vmem] * 4,
        scratch_shapes=scratch,
        compiler_params=pltpu.CompilerParams(
            collective_id=0, has_side_effects=True, vmem_limit_bytes=40 * 1024 * 1024
        ),
    )(
        state, cotangent, elem_count, face_src.reshape(1, -1), face_orient.reshape(1, -1),
        send_face.reshape(1, -1), vol_weight, w1, b1, w2, jnp.asarray(constant),
    )


def solution(mesh):
    rows, flat, whole = P("dom", None), P("dom"), P()
    return jax.shard_map(
        functools.partial(local, mesh.shape["dom"]),
        mesh=mesh,
        in_specs=(rows, rows, flat, flat, flat, flat, whole, whole, whole, whole),
        out_specs=(rows, whole, whole, whole),
        check_vma=False,
    )
```

time: 625 us -> 87 us (0.14)
  the two profiles are of different devices: /device:TPU:30 before, /device:TPU:0 now
where the time goes in v1:
time: 87 us; the launch traced here: 85.5 us
  Pallas kernels  75.6 us (87%)
  local copies, waits for them, and re-layouts  8.53 us (10%)
  between operations  1.37 us (2%)
    pallas_call x1, Pallas kernels, local(): pl.pallas_call(functools.partial(kernel, count), out_shape=(jax.ShapeDtyp...  75.6 us
    unnamed x18, local copies, waits for them, and re-layouts  6.48 us

profile of v1, /device:TPU:0, one launch (start us, length us, event | category | flops | bytes accessed | tf_op | source)
XLA Modules:
  0.0 85.5 jit_solution(15798125711444202991)
XLA Ops:
  0.6 0.0 copy-start.2
  1.3 0.7 reshape.17.src_ref
  2.0 0.7 reshape.18.orient_ref
  2.7 0.0 copy-start.5
  2.7 0.0 copy-start.6
  2.7 0.9 %copy.15.w2_ref = f32[2,64,32]{2,1,0:T(8,128)S(1)} copy(f32[2,64,32]{1,2,0:T(8,128)} %param.20) | data formatting | bytes 32768 | tf_op args[9]
  3.6 0.0 copy-done.2
  3.6 0.0 copy-done.5
  3.6 0.0 copy-done.6
  3.6 0.0 copy-start
  3.6 1.0 %copy-done = f32[48,2048]{1,0:T(8,128)S(1)} copy-done((f32[48,2048]{1,0:T(8,128)S(1)}, f32[48,2048]{1,0:T(8,128)}, u32[]{:S(2)}) %copy-start) | copy-done | bytes 393240
  4.6 0.0 copy-start.1
  4.6 1.0 %copy-done.1 = f32[48,2048]{1,0:T(8,128)S(1)} copy-done((f32[48,2048]{1,0:T(8,128)S(1)}, f32[48,2048]{1,0:T(8,128)}, u32[]{:S(2)}) %copy-start.1) | copy-done | bytes 393240
  5.6 0.0 copy-start.3
  5.6 0.8 copy-done.3
  6.4 0.0 copy-start.4
  6.4 0.8 copy-done.4
  7.3 75.6 %shard_map.138 = (f32[48,2048]{1,0:T(8,128)S(1)}, f32[2,64,64]{2,1,0:T(8,128)S(1)}, f32[2,64]{1,0:T(2,128)S(1)}, f32[2,64,32]{2,1,0:T(8,128)S(1)}) custom-call(f32[48,2048]{1,0:T(8,128)S(1)} %copy-done, f32[48,2048]{1,0:T(8,128)S(1)} %copy-done.1, s32[1]{0:T(128)S(6)} %copy.20.live_ref, s32[1,288]{1,0:T(1,128)S(1)} %reshape.17.src_ref, ...), custom_call_target="tpu_custom_call" | custom-call | tf_op jit(solution)/shard_map/pallas_call | solution.py:527
  82.9 0.7 copy.16
  83.6 0.7 copy.21
  84.4 0.6 copy.22
  85.0 0.6 copy.23
Async XLA Ops:
  0.6 2.9 %copy-start.2 = (f32[2,3,32,32]{3,2,1,0:T(8,128)S(1)}, f32[2,3,32,32]{3,2,1,0:T(8,128)}, u32[]{:S(2)}) copy-start(f32[2,3,32,32]{3,2,1,0:T(8,128)} %vol_ref.1) | copy-start | bytes 73732
  2.7 0.9 %copy-start.5 = (s32[256]{0:T(256)S(1)}, s32[256]{0:T(256)}, u32[]{:S(2)}) copy-start(s32[256]{0:T(256)} %param.16) | copy-start | bytes 3076
  2.7 0.9 %copy-start.6 = (f32[2,64]{1,0:T(2,128)S(1)}, f32[2,64]{1,0:T(2,128)}, u32[]{:S(2)}) copy-start(f32[2,64]{1,0:T(2,128)} %b1_ref.1) | copy-start | bytes 1540
  3.6 1.0 %copy-start = (f32[48,2048]{1,0:T(8,128)S(1)}, f32[48,2048]{1,0:T(8,128)}, u32[]{:S(2)}) copy-start(f32[48,2048]{1,0:T(8,128)} %state_ref.1) | copy-start | bytes 1179652
  4.6 1.0 %copy-start.1 = (f32[48,2048]{1,0:T(8,128)S(1)}, f32[48,2048]{1,0:T(8,128)}, u32[]{:S(2)}) copy-start(f32[48,2048]{1,0:T(8,128)} %cot_ref.1) | copy-start | bytes 1179652
  5.6 0.8 copy-start.3
  6.4 0.8 copy-start.4

commit v2 on v0

v2 whole, which is shorter than its diff:
```python
import functools
import types

import jax
import jax.numpy as jnp
import numpy as np
from jax import lax
from jax.experimental import pallas as pl
from jax.experimental.pallas import tpu as pltpu
from jax.sharding import PartitionSpec as P

MESH = pl.DeviceIdType.MESH
HIGHEST = lax.Precision.HIGHEST
F32 = jnp.float32
BF16 = jnp.bfloat16
I32 = jnp.int32
NEIGH = 4
BLOCKS = 2 * NEIGH
CAP = 32
SLOTS = BLOCKS * CAP
STEP_SIZE = 0.25
E = 48
FACES = 6 * E
OFFSETS = [level + 1 for level in range(NEIGH)] + [-(level + 1) for level in range(NEIGH)]


VMEM_LIMIT = 56 * 1024 * 1024


def deriv_matrix():
    points = np.array([-1.0, -np.sqrt(0.2), np.sqrt(0.2), 1.0])
    weights = np.array(
        [np.prod([points[r] - points[o] for o in range(4) if o != r]) for r in range(4)]
    )
    matrix = np.zeros((4, 4))
    for r in range(4):
        for c in range(4):
            if r != c:
                matrix[r, c] = weights[r] / weights[c] / (points[r] - points[c])
        matrix[r, r] = -np.sum(matrix[r])
    return matrix


DERIV = deriv_matrix()


def iota(shape, dim):
    return lax.broadcasted_iota(I32, shape, dim)


def dot(a, b):
    return jnp.dot(a, b, preferred_element_type=F32)


def dot_nt(a, b):
    return lax.dot_general(a, b, (((1,), (1,)), ((), ())), preferred_element_type=F32)


def dot_tn(a, b):
    return lax.dot_general(a, b, (((0,), (0,)), ((), ())), preferred_element_type=F32)


def dot_full(a, b):
    return jnp.dot(a, b, preferred_element_type=F32, precision=HIGHEST)


def split(x):
    high = x.astype(BF16)
    return high, (x - high.astype(F32)).astype(BF16)


def three(op, a, b):
    return op(a[0], b[0]) + op(a[1], b[0]) + op(a[0], b[1])


def lanes(a):
    return pl.ds(pl.multiple_of(a * 128, 128), 128)


def ones_where(match, dtype=F32):
    return jnp.where(match, 1.0, 0.0).astype(dtype)


MASKS = 4

INPUTS = ("state", "cot", "live", "src", "orient", "send", "vol", "w1", "b1", "w2t", "deriv")
OUTPUTS = ("out", "total")
SCRATCH = dict(
    src_v=((FACES,), I32), orient_v=((FACES,), I32), send_v=((1, SLOTS), I32), state_v=((E, 2048), F32), cot_v=((E, 2048), F32),
    vol_v=((2, 3, 32, 32), F32), w1_v=((2, 64, 64), F32), b1_v=((2, 64), F32), w2t_v=((2, 32, 64), F32), deriv_v=((128, 128), F32),
    out_v=((E, 2048), F32), field=((E, 2048), F32), grad=((E, 2048), F32), volume=((E, 2048), F32),
    vol_y=((16 * E, 384), F32), vol_x=((16 * E, 256), BF16),
    trace=((FACES, 1024), BF16), raw=((FACES, 512), F32),
    pair_nh=((2, FACES, 1024), BF16), pair_nl=((2, FACES, 1024), BF16), pair_fh=((2, SLOTS, 1024), BF16), pair_fl=((2, SLOTS, 1024), BF16),
    hid_nh=((2, FACES, 1024), BF16), hid_nl=((2, FACES, 1024), BF16), hid_fh=((2, SLOTS, 1024), BF16), hid_fl=((2, SLOTS, 1024), BF16),
    flux=((FACES, 512), F32), flux_fh=((SLOTS, 512), BF16), flux_fl=((SLOTS, 512), BF16),
    gflux=((FACES, 1024), BF16), gflux_n=((FACES, 1024), BF16), gflux_f=((SLOTS, 1024), BF16), ghid_f=((SLOTS, 1024), F32),
    gpre_nh=((FACES, 1024), BF16), gpre_nl=((FACES, 1024), BF16), gpre_fh=((SLOTS, 1024), BF16), gpre_fl=((SLOTS, 1024), BF16),
    gin=((FACES, 512), F32), gin_fh=((SLOTS, 512), BF16), gin_fl=((SLOTS, 512), BF16), gout=((FACES, 512), F32),
    turn=((FACES, 1024), BF16),
    sel=((SLOTS, FACES), BF16), sel_t=((FACES, SLOTS), BF16), loc=((FACES, FACES), BF16), loc_t=((FACES, FACES), BF16),
    rem=((FACES, SLOTS), BF16), rem_t=((SLOTS, FACES), BF16),
    masks_n=((FACES, MASKS * 128), F32), masks_f=((SLOTS, MASKS * 128), F32),
    w1h=((2, 256, 256), BF16), w1l=((2, 256, 256), BF16), w1th=((2, 256, 256), BF16), w1tl=((2, 256, 256), BF16),
    w2c=((2, 256, 256), BF16), w2ts=((2, 256, 256), BF16), w2tl=((2, 128, 256), BF16),
    vs=((2, 256, 384), BF16), vl=((2, 128, 384), BF16), vts=((2, 256, 384), BF16), vtl=((2, 128, 384), BF16), bias=((2, 8, 256), F32),
    sent=((4, SLOTS, 512), F32), got=((4, SLOTS, 512), F32),
    one=((256, 256), F32), two=((256, 128), F32), row=((8, 256), F32),
    packed=((2, 64, 128), F32), part=((2, 8, 8, 128), F32),
)


def kernel(count, names, *refs):
    s = types.SimpleNamespace(**dict(zip(names, refs, strict=True)))
    me = lax.axis_index("dom")
    group = 8
    others = count // group
    base = (me // group) * group
    mine = lax.rem(me, group)
    rank = me // group

    def neighbour(offset):
        return lax.rem(me + offset + count, count)

    def in_group(step):
        return base + lax.rem(mine + step, group)

    def across(step):
        return lax.rem(rank + step, others) * group + mine

    barrier = pltpu.get_barrier_semaphore()
    partners = [neighbour(o) for o in OFFSETS]
    partners += [in_group(step) for step in range(1, group)]
    partners += [across(step) for step in range(1, others)]
    for device in partners:
        pl.semaphore_signal(barrier, inc=1, device_id=(device,), device_id_type=MESH)

    pulls = {}
    for n, name in enumerate(("send", "state", "live", "src", "orient", "vol", "w1", "b1", "w2t", "deriv", "cot")):
        pulls[name] = pltpu.make_async_copy(getattr(s, name), getattr(s, name + "_v"), s.in_sem.at[n])
        pulls[name].start()

    def far_copy(which, pair, side, sign):
        rows = pl.ds(pl.multiple_of(64 * pair + CAP * side, CAP), CAP)
        offset = (pair + 1) * (sign if side == 0 else -sign)
        return pltpu.make_async_remote_copy(
            src_ref=s.sent.at[which, rows],
            dst_ref=s.got.at[which, rows],
            send_sem=s.send_sem.at[which, 2 * pair + side],
            recv_sem=s.recv_sem.at[which, 2 * pair + side],
            device_id=(neighbour(offset),),
            device_id_type=MESH,
        )

    def send_all(which, sign):
        for pair in (3, 2, 1, 0):
            for side in range(2):
                far_copy(which, pair, side, sign).start()

    def wait_all(which, sign):
        for pair in (3, 2, 1, 0):
            for side in range(2):
                far_copy(which, pair, side, sign).wait_recv()

    def wait_sent(which, sign):
        for pair in (3, 2, 1, 0):
            for side in range(2):
                far_copy(which, pair, side, sign).wait_send()

    def tile(ref, n):
        return ref[:, n * 128 : (n + 1) * 128]

    def wide(a):
        return slice(256 * a, 256 * a + 256)

    def high(a):
        return slice(256 * a, 256 * a + 128)

    def low(a):
        return slice(256 * a + 128, 256 * a + 256)

    def narrow(a):
        return slice(128 * a, 128 * a + 128)

    group_of_lane = iota((E, 128), 1) >> 5

    def traces(ref, emit):
        for a in range(4):
            emit(0, a, tile(ref, a))
            emit(1, a, tile(ref, 12 + a))
            emit(2, a, tile(ref, 4 * a))
            emit(3, a, tile(ref, 4 * a + 3))
            first = tile(ref, 4 * a)
            last = pltpu.roll(tile(ref, 4 * a), 32, 1)
            for b in range(1, 4):
                node = tile(ref, 4 * a + b)
                first = jnp.where(group_of_lane == b, pltpu.roll(node, 32 * b, 1), first)
                moved = node if b == 3 else pltpu.roll(node, 32 * (b + 1), 1)
                last = jnp.where(group_of_lane == b, moved, last)
            emit(4, a, first)
            emit(5, a, last)

    def lift(ref, i, j):
        at = lambda f, a: ref[f * E : (f + 1) * E, narrow(a)]
        first, last = at(4, i), at(5, i)
        first = pltpu.roll(first, (128 - 32 * j) % 128, 1) if j else first
        last = pltpu.roll(last, 96 - 32 * j, 1) if j < 3 else last
        value = jnp.where(group_of_lane == 0, first, jnp.where(group_of_lane == 3, last, 0.0))
        if i == 0:
            value = value + at(0, j)
        if i == 3:
            value = value + at(1, j)
        if j == 0:
            value = value + at(2, i)
        if j == 3:
            value = value + at(3, i)
        return value

    def keep_traces(layer):
        def emit(f, a, value):
            h, l = split(value)
            rows = slice(f * E, (f + 1) * E)
            s.trace[rows, narrow(a)] = h
            s.trace[rows, slice(512 + 128 * a, 640 + 128 * a)] = l
            s.pair_nh[layer, rows, high(a)] = h
            s.pair_nl[layer, rows, high(a)] = l

        return emit

    def keep_gflux(masked):
        def emit(f, a, value):
            h, l = split(STEP_SIZE * value)
            rows = slice(f * E, (f + 1) * E)
            s.gflux[rows, high(a)] = h
            s.gflux[rows, low(a)] = l
            if masked:
                here = s.masks_n[rows, 384:512].astype(BF16)
                s.gflux_n[rows, high(a)] = h * here
                s.gflux_n[rows, low(a)] = l * here

        return emit

    def gathered(matrix, ref):
        both = dot(matrix[...], ref[...])
        return both[:, 0:512] + both[:, 512:1024]

    def volume_of(ref, layer, adjoint):
        for n in range(16):
            h, l = split(tile(ref, n))
            s.vol_x[n * E : (n + 1) * E, 0:128] = h
            s.vol_x[n * E : (n + 1) * E, 128:256] = l
        stacked, rest = (s.vts, s.vtl) if adjoint else (s.vs, s.vl)
        s.vol_y[...] = dot(s.vol_x[...], stacked[layer]) + dot(s.vol_x[:, 0:128], rest[layer])
        deriv = DERIV.T if adjoint else DERIV
        for i in range(4):
            for j in range(4):
                n = 4 * i + j
                value = s.vol_y[n * E : (n + 1) * E, 256:384]
                for o in range(4):
                    if abs(deriv[i, o]) > 1e-12:
                        at = 4 * o + j
                        value = value + float(deriv[i, o]) * s.vol_y[at * E : (at + 1) * E, 0:128]
                    if abs(deriv[j, o]) > 1e-12:
                        at = 4 * i + o
                        value = value + float(deriv[j, o]) * s.vol_y[at * E : (at + 1) * E, 128:256]
                s.volume[:, narrow(n)] = value

    def flip_lanes(x, odd):
        return jnp.where(odd, pltpu.roll(x, 96, 1), pltpu.roll(x, 32, 1))

    def swap(x, odd, upper):
        stage = [None] * 4
        for a in (0, 2):
            stage[a] = jnp.where(odd, pltpu.roll(x[a + 1], 32, 1), x[a])
            stage[a + 1] = jnp.where(odd, x[a + 1], pltpu.roll(x[a], 96, 1))
        out = [None] * 4
        for a in (0, 1):
            out[a] = jnp.where(upper, pltpu.roll(stage[a + 2], 64, 1), stage[a])
            out[a + 2] = jnp.where(upper, stage[a + 2], pltpu.roll(stage[a], 64, 1))
        return out

    def lane_masks(count_):
        groups = iota((count_, 128), 1) >> 5
        return (groups & 1) == 1, groups >= 2

    def oriented(x, marks):
        odd, upper = lane_masks(x[0].shape[0])
        first, second, swapped = marks
        x = [jnp.where(first, x[3 - a], x[a]) for a in range(4)]
        x = [jnp.where(second, flip_lanes(v, odd), v) for v in x]
        y = swap(x, odd, upper)
        return [jnp.where(swapped, y[a], x[a]) for a in range(4)]

    def turned_back(x, marks):
        odd, upper = lane_masks(x[0].shape[0])
        first, second, swapped = marks
        y = swap(x, odd, upper)
        x = [jnp.where(swapped, y[a], x[a]) for a in range(4)]
        x = [jnp.where(second, flip_lanes(v, odd), v) for v in x]
        return [jnp.where(first, x[3 - a], x[a]) for a in range(4)]

    def marks_of(ref, rows):
        return [ref[rows, narrow(m)] > 0.5 for m in range(3)]

    def each_rows(body):
        body(slice(0, FACES))

    def orient_near(layer):
        def body(rows):
            x = oriented([s.raw[rows, narrow(a)] for a in range(4)], marks_of(s.masks_n, rows))
            for a in range(4):
                s.pair_nh[layer, rows, low(a)], s.pair_nl[layer, rows, low(a)] = split(x[a])

        each_rows(body)

    def turn_back_near():
        def body(rows):
            x = turned_back([s.gout[rows, narrow(a)] for a in range(4)], marks_of(s.masks_n, rows))
            for a in range(4):
                h, l = split(x[a])
                s.turn[rows, narrow(a)] = h
                s.turn[rows, slice(512 + 128 * a, 640 + 128 * a)] = l

        each_rows(body)

    def each_a(body):
        for a in range(4):
            body(wide(a), high(a), narrow(a))

    def hidden(xh, xl, layer):
        pre = dot(xh, s.w1h[layer]) + dot(xl, s.w1h[layer]) + dot(xh, s.w1l[layer])
        return jnp.tanh(pre + s.bias[layer, 0:1, :])

    def flux_of(h, l, layer):
        both = dot(h, s.w2c[layer])
        return both[:, 0:128] + both[:, 128:256] + dot(l, s.w2c[layer, :, 0:128])

    def hidden_grad(both, top, layer):
        return dot(both, s.w2ts[layer]) + dot(top, s.w2tl[layer])

    def pair_grad(h, l, layer):
        return dot(h, s.w1th[layer]) + dot(l, s.w1th[layer]) + dot(h, s.w1tl[layer])

    def hidden_near(layer):
        def body(w, h_, n):
            h, l = split(hidden(s.pair_nh[layer, :, w], s.pair_nl[layer, :, w], layer))
            s.hid_nh[layer, :, w] = h
            s.hid_nl[layer, :, w] = l
            if layer == 0:
                s.flux[:, n] = flux_of(h, l, layer) * s.masks_n[:, 384:512]

        each_a(body)

    def back_near(layer, gflux):
        def body(w, h_, n):
            h = s.hid_nh[layer, :, w].astype(F32) + s.hid_nl[layer, :, w].astype(F32)
            gp = hidden_grad(gflux[:, w], gflux[:, h_], layer) * (1.0 - h * h)
            gh, gl = split(gp)
            s.gpre_nh[:, w] = gh
            s.gpre_nl[:, w] = gl
            both = pair_grad(gh, gl, layer)
            s.gin[:, n] = both[:, 0:128]
            s.gout[:, n] = both[:, 128:256]

        each_a(body)

    def far_pairs(which, layer):
        def step(n, carry):
            pair = 3 - n
            rows = pl.ds(pl.multiple_of(64 * pair, 64), 64)
            for side in range(2):
                far_copy(which, pair, side, 1).wait_recv()
            for side in range(2):
                part_rows = pl.ds(pl.multiple_of(64 * pair + CAP * side, CAP), CAP)
                x = oriented([s.got[which, part_rows, narrow(a)] for a in range(4)], marks_of(s.masks_f, part_rows))
                for a in range(4):
                    s.pair_fh[layer, part_rows, low(a)], s.pair_fl[layer, part_rows, low(a)] = split(x[a])
            stack = lambda ref, cut: jnp.concatenate([ref[rows, cut(a)] for a in range(4)], axis=0)
            value = hidden(stack(s.pair_fh.at[layer], wide), stack(s.pair_fl.at[layer], wide), layer)
            h, l = split(value)
            part_of = lambda v, a: v[64 * a : 64 * a + 64]
            for a in range(4):
                s.hid_fh[layer, rows, wide(a)] = part_of(h, a)
                s.hid_fl[layer, rows, wide(a)] = part_of(l, a)
            if layer == 0:
                fh, fl = split(flux_of(h, l, layer))
                for a in range(4):
                    s.flux_fh[rows, narrow(a)] = part_of(fh, a)
                    s.flux_fl[rows, narrow(a)] = part_of(fl, a)
            else:
                gh, gl = split(stack(s.ghid_f, wide) * (1.0 - value * value))
                both = pair_grad(gh, gl, layer)
                ih, il = split(both[:, 0:128])
                for a in range(4):
                    s.gpre_fh[rows, wide(a)] = part_of(gh, a)
                    s.gpre_fl[rows, wide(a)] = part_of(gl, a)
                    s.gin_fh[rows, narrow(a)] = part_of(ih, a)
                    s.gin_fl[rows, narrow(a)] = part_of(il, a)
                for side in range(2):
                    part_rows = pl.ds(pl.multiple_of(64 * pair + CAP * side, CAP), CAP)
                    cut = lambda a: both[64 * a + CAP * side : 64 * a + CAP * side + CAP, 128:256]
                    x = turned_back([cut(a) for a in range(4)], marks_of(s.masks_f, part_rows))
                    for a in range(4):
                        s.sent[which + 1, part_rows, narrow(a)] = x[a]
                for side in range(2):
                    far_copy(which + 1, pair, side, -1).start()
            return carry

        lax.fori_loop(0, 4, step, 0)

    def far_inner(layer):
        both = dot(s.rem_t[...], s.trace[...]).astype(BF16)
        for a in range(4):
            s.pair_fh[layer, :, high(a)] = both[:, narrow(a)]
            s.pair_fl[layer, :, high(a)] = both[:, 512 + 128 * a : 640 + 128 * a]

    def weight_grads(parts):
        rows_of = lambda ref, cut: jnp.concatenate([ref[:, cut(a)] for a in range(4)], axis=0)
        xh, xl, gph, gpl, hh, hl, g = parts
        gh, gl, x = rows_of(gph, wide), rows_of(gpl, wide), rows_of(xh, wide)
        one = dot_tn(x, gh) + dot_tn(rows_of(xl, wide), gh) + dot_tn(x, gl)
        two = dot_tn(rows_of(hh, wide), rows_of(g, wide))
        top = dot_tn(rows_of(hl, wide), rows_of(g, high))
        two = two[:, 0:128] + two[:, 128:256] + top
        row = jnp.sum(gh.astype(F32) + gl.astype(F32), axis=0, keepdims=True)
        return one, two, row

    def pack_grads(layer, one, two, row):
        r, c = iota((256, 256), 0), iota((256, 256), 1)
        one = jnp.where(((r >> 5) & 3) == (c >> 6), one, 0.0)
        one = one[:, 0:128] + one[:, 128:256]
        one = one + pltpu.roll(one, 64, 1)
        halves = [sum(one[128 * half + 32 * b : 128 * half + 32 * b + 32] for b in range(4)) for half in range(2)]
        one = jnp.concatenate(halves, axis=0)
        r, c = iota((256, 128), 0), iota((256, 128), 1)
        two = jnp.where((r >> 6) == (c >> 5), two, 0.0)
        two = sum(two[64 * b : 64 * b + 64] for b in range(4))
        two = two + pltpu.roll(two, 64, 1)
        two = two + pltpu.roll(two, 32, 1)
        row = row[:, 0:128] + row[:, 128:256]
        row = row + pltpu.roll(row, 64, 1)
        r, c = iota((64, 128), 0), iota((64, 128), 1)
        column = jnp.sum(jnp.where(r == c, row, 0.0), axis=1, keepdims=True)
        value = jnp.where(c < 64, one, jnp.where(c < 96, two, jnp.where(c == 96, column, 0.0)))
        s.packed[layer] = value

    def piece(j):
        return pl.ds(pl.multiple_of(j * 8, 8), 8)

    def remote(src, dst, sems, device):
        return pltpu.make_async_remote_copy(
            src_ref=src, dst_ref=dst, send_sem=sems[0], recv_sem=sems[1], device_id=(device,), device_id_type=MESH
        )

    def sems(layer, stage, step):
        return s.ar_send.at[layer, stage, step], s.ar_recv.at[layer, stage, step]

    def scatter(layer):
        return [
            remote(s.packed.at[layer, piece(lax.rem(mine + t, group))], s.part.at[layer, mine], sems(layer, 0, t), in_group(t))
            for t in range(1, group)
        ]

    def spread(layer):
        here = s.part_sum.at[layer, rank]
        return [remote(here, here, sems(layer, 1, t), across(t)) for t in range(1, others)]

    def collect(layer):
        here = s.total_v.at[layer, piece(mine)]
        return [remote(here, here, sems(layer, 2, t), in_group(t)) for t in range(1, group)]

    def start(copies):
        for copy in copies:
            copy.start()

    def wait(copies):
        for copy in copies:
            copy.wait()

    def reduce_start(layer):
        start(scatter(layer))
        s.part[layer, mine] = s.packed[layer, piece(mine), :]

    def reduce_middle(layer):
        wait(scatter(layer))
        value = s.part[layer, 0]
        for t in range(1, group):
            value = value + s.part[layer, t]
        s.part_sum[layer, rank] = value
        start(spread(layer))

    def reduce_last(layer):
        wait(spread(layer))
        value = s.part_sum[layer, 0]
        for t in range(1, others):
            value = value + s.part_sum[layer, t]
        s.total_v[layer, piece(mine), :] = value
        start(collect(layer))

    with jax.named_scope("send_table"):
        order = (0, 4, 1, 5, 2, 6, 3, 7)
        pulls["send"].wait()
        row = s.send_v[...]
        row = jnp.concatenate([row[:, CAP * b : CAP * b + CAP] for b in order], axis=1)
        for f in range(6):
            s.sel_t[f * E : (f + 1) * E, :] = ones_where(6 * iota((E, SLOTS), 0) + f == row, BF16)
        eye = ones_where(iota((SLOTS, SLOTS), 0) == iota((SLOTS, SLOTS), 1), BF16)
        s.sel[...] = dot_nt(eye, s.sel_t[...]).astype(BF16)

    with jax.named_scope("field0"):
        pulls["state"].wait()
        pulls["live"].wait()
        alive = iota((E, 128), 0) < s.live_v[0]
        for n in range(16):
            s.field[:, narrow(n)] = jnp.where(alive, tile(s.state_v, n), 0.0)
        traces(s.field, keep_traces(0))
    with jax.named_scope("pack0"):
        s.sent[0] = gathered(s.sel, s.trace)
    with jax.named_scope("barrier"):
        pl.semaphore_wait(barrier, len(partners))
    send_all(0, 1)

    with jax.named_scope("tables"):
        for f in range(6):
            s.raw[f * E : (f + 1) * E, 0:FACES] = ones_where(6 * iota((E, FACES), 0) + f == iota((E, FACES), 1))
        by_kind = s.raw[:, 0:FACES].astype(BF16)
        pulls["src"].wait()
        source = s.src_v[...].reshape(1, FACES)
        near = jnp.concatenate([ones_where(6 * iota((E, FACES), 0) + f == source, BF16) for f in range(6)], axis=0)
        slot = iota((SLOTS, FACES), 0)
        slot = ((slot >> 5) & 1) * 128 + (slot >> 6) * CAP + (slot & 31)
        far = ones_where(slot + FACES == source, BF16)
        s.loc_t[...] = dot_nt(near, by_kind).astype(BF16)
        s.loc[...] = dot_nt(by_kind, near).astype(BF16)
        s.rem_t[...] = dot_nt(far, by_kind).astype(BF16)
        s.rem[...] = dot_nt(by_kind, far).astype(BF16)
        pulls["orient"].wait()
        turn = s.orient_v[...].reshape(1, FACES)
        flags = [(turn >> 1) & 1, (turn ^ (turn >> 1)) & 1, (turn ^ (turn >> 2)) & 1, jnp.where(source < FACES, 1, 0)]
        for m in range(MASKS):
            spread_out = jnp.broadcast_to(flags[m], (128, FACES)).astype(F32).astype(BF16)
            s.masks_n[:, narrow(m)] = dot_nt(by_kind, spread_out)
            s.masks_f[:, narrow(m)] = dot_nt(far, spread_out)

    def four(x):
        x = jnp.concatenate([x] * 4, axis=1)
        return jnp.concatenate([x] * 4, axis=0)

    def flux_weights(layer):
        r, c = iota((256, 256), 0), iota((256, 256), 1)
        w1 = s.w1_v[layer]
        big = jnp.concatenate([four(w1[0:32]), four(w1[32:64])], axis=0)
        big = jnp.where(((r >> 5) & 3) == (c >> 6), big, 0.0)
        s.w1h[layer], s.w1l[layer] = split(big)
        s.w1th[layer], s.w1tl[layer] = split(big.T)
        r, c = iota((128, 256), 0), iota((128, 256), 1)
        big = jnp.where((r >> 5) == (c >> 6), four(s.w2t_v[layer]), 0.0)
        h, l = split(big)
        s.w2ts[layer, 0:128] = h
        s.w2ts[layer, 128:256] = h
        s.w2tl[layer] = l
        h, l = split(big.T)
        s.w2c[layer, :, 0:128] = h
        s.w2c[layer, :, 128:256] = l
        bias = jnp.concatenate([s.b1_v[layer : layer + 1, :]] * 4, axis=1)
        s.bias[layer] = jnp.broadcast_to(bias, (8, 256))

    def volume_weights(layer):
        r, c = iota((128, 128), 0), iota((128, 128), 1)
        for axis in range(3):
            big = four(s.vol_v[layer, axis])
            big = jnp.where((r >> 5) == (c >> 5), big, 0.0) if axis < 2 else big * s.deriv_v[...]
            for value, stacked, rest in ((big, s.vs, s.vl), (big.T, s.vts, s.vtl)):
                h, l = split(value)
                stacked[layer, 0:128, narrow(axis)] = h
                stacked[layer, 128:256, narrow(axis)] = h
                rest[layer, :, narrow(axis)] = l

    with jax.named_scope("weights0"):
        for name in ("w1", "w2t", "b1", "vol", "deriv"):
            pulls[name].wait()
        flux_weights(0)
        volume_weights(0)
    with jax.named_scope("near0"):
        s.raw[...] = gathered(s.loc, s.trace)
        far_inner(0)
    with jax.named_scope("orient0"):
        orient_near(0)
    with jax.named_scope("hidden0"):
        hidden_near(0)
    with jax.named_scope("volume0"):
        volume_of(s.field, 0, False)
    with jax.named_scope("weights1"):
        flux_weights(1)
    with jax.named_scope("cotangent"):
        pulls["cot"].wait()
        traces(s.cot_v, keep_gflux(True))
    with jax.named_scope("cotangent_far"):
        s.gflux_f[...] = dot(s.rem_t[...], s.gflux[...]).astype(BF16)
        for a in range(4):
            s.ghid_f[:, wide(a)] = hidden_grad(s.gflux_f[:, wide(a)], s.gflux_f[:, high(a)], 1)
    with jax.named_scope("far0"):
        far_pairs(0, 0)
    with jax.named_scope("field1"):
        s.flux[...] += dot(s.rem[...], s.flux_fh[...]) + dot(s.rem[...], s.flux_fl[...])
        for n in range(16):
            s.field[:, narrow(n)] += STEP_SIZE * (lift(s.flux, n // 4, n % 4) - s.volume[:, narrow(n)])
        traces(s.field, keep_traces(1))
    with jax.named_scope("pack1"):
        s.sent[1] = gathered(s.sel, s.trace)
    send_all(1, 1)
    with jax.named_scope("near1"):
        s.raw[...] = gathered(s.loc, s.trace)
        far_inner(1)
    with jax.named_scope("orient1"):
        orient_near(1)
    with jax.named_scope("hidden1"):
        hidden_near(1)
    with jax.named_scope("back1"):
        back_near(1, s.gflux_n)
    with jax.named_scope("whole0"):
        for far, here in ((s.pair_fh, s.pair_nh), (s.pair_fl, s.pair_nl)):
            value = dot(s.rem[...], jnp.concatenate([far[0, :, low(a)] for a in range(4)], axis=1)).astype(BF16)
            for a in range(4):
                here[0, :, low(a)] += value[:, narrow(a)]
        for far, here in ((s.hid_fh, s.hid_nh), (s.hid_fl, s.hid_nl)):
            for a in range(4):
                own = s.masks_n[:, 384:512].astype(BF16)
                value = dot(s.rem[...], far[0, :, wide(a)]).astype(BF16)
                here[0, :, wide(a)] = here[0, :, wide(a)] * jnp.concatenate([own, own], axis=1) + value
    with jax.named_scope("weight_grads1_near"):
        parts = s.pair_nh.at[1], s.pair_nl.at[1], s.gpre_nh, s.gpre_nl, s.hid_nh.at[1], s.hid_nl.at[1], s.gflux_n
        s.one[...], s.two[...], row = weight_grads(parts)
        s.row[...] = jnp.broadcast_to(row, (8, 256))
    with jax.named_scope("far1"):
        far_pairs(1, 1)

    with jax.named_scope("turn1"):
        turn_back_near()
    with jax.named_scope("scatter1"):
        both = dot(s.loc_t[...], s.turn[...])
        value = both[:, 0:512] + both[:, 512:1024]
        s.gin[...] += value + dot(s.rem[...], s.gin_fh[...]) + dot(s.rem[...], s.gin_fl[...])
    with jax.named_scope("volume1"):
        volume_weights(1)
        volume_of(s.cot_v, 1, True)
    with jax.named_scope("weight_grads1"):
        parts = s.pair_fh.at[1], s.pair_fl.at[1], s.gpre_fh, s.gpre_fl, s.hid_fh.at[1], s.hid_fl.at[1], s.gflux_f
        one, two, row = weight_grads(parts)
        pack_grads(1, one + s.one[...], two + s.two[...], row + s.row[0:1, :])
        reduce_start(1)
    with jax.named_scope("wait2"):
        wait_all(2, -1)
    with jax.named_scope("grad1"):
        h, l = split(s.got[2])
        s.gin[...] += dot(s.sel_t[...], h) + dot(s.sel_t[...], l)
        for n in range(16):
            s.grad[:, narrow(n)] = tile(s.cot_v, n) - STEP_SIZE * s.volume[:, narrow(n)] + lift(s.gin, n // 4, n % 4)
        traces(s.grad, keep_gflux(False))
    with jax.named_scope("back0"):
        back_near(0, s.gflux)
    with jax.named_scope("weight_grads0"):
        parts = s.pair_nh.at[0], s.pair_nl.at[0], s.gpre_nh, s.gpre_nl, s.hid_nh.at[0], s.hid_nl.at[0], s.gflux
        pack_grads(0, *weight_grads(parts))
        reduce_start(0)
    with jax.named_scope("turn0"):
        turn_back_near()
    with jax.named_scope("pack3"):
        s.sent[3] = gathered(s.rem_t, s.turn)
    send_all(3, -1)
    with jax.named_scope("sum1a"):
        reduce_middle(1)
    with jax.named_scope("sum0a"):
        reduce_middle(0)
    with jax.named_scope("scatter0"):
        both = dot(s.loc_t[...], s.turn[...])
        s.gin[...] += both[:, 0:512] + both[:, 512:1024]
    with jax.named_scope("volume0b"):
        volume_of(s.grad, 0, True)
    with jax.named_scope("sum1b"):
        reduce_last(1)
    with jax.named_scope("sum0b"):
        reduce_last(0)
    with jax.named_scope("wait3"):
        wait_all(3, -1)
    with jax.named_scope("grad0"):
        h, l = split(s.got[3])
        s.gin[...] += dot(s.sel_t[...], h) + dot(s.sel_t[...], l)
        for n in range(16):
            value = s.grad[:, narrow(n)] - STEP_SIZE * s.volume[:, narrow(n)] + lift(s.gin, n // 4, n % 4)
            s.out_v[:, narrow(n)] = jnp.where(alive, value, 0.0)
        push = pltpu.make_async_copy(s.out_v, s.out, s.out_sem.at[0])
        push.start()
    with jax.named_scope("sumc"):
        wait(collect(1))
        wait(collect(0))
        push_total = pltpu.make_async_copy(s.total_v, s.total, s.out_sem.at[1])
        push_total.start()
    with jax.named_scope("sent"):
        wait_sent(0, 1)
        wait_sent(1, 1)
        wait_sent(2, -1)
        wait_sent(3, -1)
        push.wait()
        push_total.wait()


def finish(factor, total_ref, field_ref, out_ref, w1_ref, b1_ref, w2t_ref):
    out_ref[...] = field_ref[...]
    for layer in range(2):
        value = total_ref[layer] * factor
        w1_ref[layer] = value[:, 0:64]
        w2t_ref[layer] = value.T[64:96, :]
        b1_ref[layer : layer + 1, :] = value.T[96:97, :]


def local(count, state, cotangent, elem_count, face_src, face_orient, send_face, vol_weight, w1, b1, w2):
    constant = np.zeros((128, 128), np.float32)
    for a in range(4):
        for k in range(4):
            constant[32 * k : 32 * k + 32, 32 * a : 32 * a + 32] = DERIV[a, k]
    vmem = pl.BlockSpec(memory_space=pltpu.VMEM)
    smem = pl.BlockSpec(memory_space=pltpu.SMEM)
    hbm = pl.BlockSpec(memory_space=pl.ANY)
    names = [*INPUTS, *OUTPUTS, *SCRATCH]
    scratch = [pltpu.VMEM(shape, dtype) for shape, dtype in SCRATCH.values()]
    extra = dict(
        part_sum=pltpu.VMEM((2, count // 8, 8, 128), F32),
        total_v=pltpu.VMEM((2, 64, 128), F32),
        live_v=pltpu.SMEM((1,), I32),
        out_sem=pltpu.SemaphoreType.DMA((2,)),
        in_sem=pltpu.SemaphoreType.DMA((11,)),
        send_sem=pltpu.SemaphoreType.DMA((4, BLOCKS)),
        recv_sem=pltpu.SemaphoreType.DMA((4, BLOCKS)),
        ar_send=pltpu.SemaphoreType.DMA((2, 3, 16)),
        ar_recv=pltpu.SemaphoreType.DMA((2, 3, 16)),
    )
    names += list(extra)
    scratch += list(extra.values())
    field, total = pl.pallas_call(
        functools.partial(kernel, count, names),
        out_shape=(jax.ShapeDtypeStruct(state.shape, F32), jax.ShapeDtypeStruct((2, 64, 128), F32)),
        in_specs=[hbm, hbm, hbm, hbm, hbm, hbm] + [hbm] * 5,
        out_specs=[hbm] * 2,
        scratch_shapes=scratch,
        compiler_params=pltpu.CompilerParams(
            collective_id=0, has_side_effects=True, vmem_limit_bytes=VMEM_LIMIT
        ),
    )(
        state, cotangent, elem_count, face_src, face_orient,
        send_face.reshape(1, -1), vol_weight, w1, b1, jnp.swapaxes(w2, 1, 2), jnp.asarray(constant),
    )
    factor = (2.0 * FACES * 8 * count) ** -0.5
    grad, grad_w1, grad_b1, grad_w2t = pl.pallas_call(
        functools.partial(finish, factor),
        out_shape=(
            jax.ShapeDtypeStruct(state.shape, F32),
            jax.ShapeDtypeStruct(w1.shape, F32),
            jax.ShapeDtypeStruct(b1.shape, F32),
            jax.ShapeDtypeStruct((2, 32, 64), F32),
        ),
        in_specs=[vmem] * 2,
        out_specs=[vmem] * 4,
    )(total, field)
    return grad, grad_w1, grad_b1, jnp.swapaxes(grad_w2t, 1, 2)


def solution(mesh):
    rows, flat, whole = P("dom", None), P("dom"), P()
    return jax.shard_map(
        functools.partial(local, mesh.shape["dom"]),
        mesh=mesh,
        in_specs=(rows, rows, flat, flat, flat, flat, whole, whole, whole, whole),
        out_specs=(rows, whole, whole, whole),
        check_vma=False,
    )
```

time: 625 us -> 62.7 us (0.10)
  the two profiles are of different devices: /device:TPU:30 before, /device:TPU:0 now
where the time goes in v2:
time: 62.7 us; the launch traced here: 61.5 us
  Pallas kernels  60.2 us (96%)
  between operations  1.29 us (2%)
    pallas_call x1, Pallas kernels, local(): pl.pallas_call(functools.partial(kernel, count, names), out_shape=(jax.Sh...  58.4 us
    pallas_call x1, Pallas kernels, local(): pl.pallas_call(functools.partial(finish, factor), out_shape=(jax.ShapeDty...  1.82 us

profile of v2, /device:TPU:0, one launch (start us, length us, event | category | flops | bytes accessed | tf_op | source)
XLA Modules:
  0.0 61.5 jit_solution(11384963170281895531)
XLA Ops:
  1.3 58.4 %shard_map.138 = (f32[48,2048]{1,0:T(8,128)}, f32[2,64,128]{2,1,0:T(8,128)}) custom-call(f32[48,2048]{1,0:T(8,128)} %refs_0_.1, f32[48,2048]{1,0:T(8,128)} %refs_1_.1, s32[1]{0:T(128)S(6)} %copy.15.refs_2_, s32[288]{0:T(512)} %refs_3_.1, s32[288]{0:T(512)} %refs_4_.1, s32[1,256]{1,0:T(1,128)} %bitcast.4, f32[2,3,32,32]{3,2,1,0:T(8,128)} %refs_6_.1, ...), custom_call_target="tpu_custom_call" | custom-call | tf_op jit(solution)/shard_map/pallas_call | solution.py:740
  59.7 1.8 %shard_map.139 = (f32[48,2048]{1,0:T(8,128)}, f32[2,64,64]{2,1,0:T(8,128)}, f32[2,64]{1,0:T(2,128)}, f32[2,32,64]{2,1,0:T(8,128)}) custom-call(f32[2,64,128]{2,1,0:T(8,128)} %get-tuple-element.10.total_ref, f32[48,2048]{1,0:T(8,128)} %get-tuple-element.11.field_ref), custom_call_target="tpu_custom_call" | custom-call | tf_op jit(solution)/shard_map/pallas_call | solution.py:754

commit v3 on v2

--- a/solution.py
+++ b/solution.py
@@ -146,8 +146,8 @@
         return pltpu.make_async_remote_copy(
             src_ref=s.sent.at[which, rows],
             dst_ref=s.got.at[which, rows],
-            send_sem=s.send_sem.at[which, 2 * pair + side],
-            recv_sem=s.recv_sem.at[which, 2 * pair + side],
+            send_sem=s.send_sem.at[which],
+            recv_sem=s.near_sem.at[which, pair] if which < 2 else s.back_sem.at[which - 2],
             device_id=(neighbour(offset),),
             device_id_type=MESH,
         )
@@ -157,15 +157,16 @@
             for side in range(2):
                 far_copy(which, pair, side, sign).start()
 
-    def wait_all(which, sign):
-        for pair in (3, 2, 1, 0):
-            for side in range(2):
-                far_copy(which, pair, side, sign).wait_recv()
-
-    def wait_sent(which, sign):
-        for pair in (3, 2, 1, 0):
-            for side in range(2):
-                far_copy(which, pair, side, sign).wait_send()
+    def all_of(which, pair=None):
+        rows = pl.ds(0, SLOTS) if pair is None else pl.ds(pl.multiple_of(64 * pair, 64), 64)
+        return pltpu.make_async_remote_copy(
+            src_ref=s.sent.at[which, rows],
+            dst_ref=s.got.at[which, rows],
+            send_sem=s.send_sem.at[which],
+            recv_sem=s.near_sem.at[which, pair] if which < 2 else s.back_sem.at[which - 2],
+            device_id=(neighbour(1),),
+            device_id_type=MESH,
+        )
 
     def tile(ref, n):
         return ref[:, n * 128 : (n + 1) * 128]
@@ -368,8 +369,7 @@
         def step(n, carry):
             pair = 3 - n
             rows = pl.ds(pl.multiple_of(64 * pair, 64), 64)
-            for side in range(2):
-                far_copy(which, pair, side, 1).wait_recv()
+            all_of(which, pair).wait_recv()
             for side in range(2):
                 part_rows = pl.ds(pl.multiple_of(64 * pair + CAP * side, CAP), CAP)
                 x = oriented([s.got[which, part_rows, narrow(a)] for a in range(4)], marks_of(s.masks_f, part_rows))
@@ -452,37 +452,41 @@
             src_ref=src, dst_ref=dst, send_sem=sems[0], recv_sem=sems[1], device_id=(device,), device_id_type=MESH
         )
 
-    def sems(layer, stage, step):
-        return s.ar_send.at[layer, stage, step], s.ar_recv.at[layer, stage, step]
+    def sems(layer, stage):
+        return s.ar_send.at[layer, stage], s.ar_recv.at[layer, stage]
 
     def scatter(layer):
         return [
-            remote(s.packed.at[layer, piece(lax.rem(mine + t, group))], s.part.at[layer, mine], sems(layer, 0, t), in_group(t))
+            remote(s.packed.at[layer, piece(lax.rem(mine + t, group))], s.part.at[layer, mine], sems(layer, 0), in_group(t))
             for t in range(1, group)
         ]
 
     def spread(layer):
         here = s.part_sum.at[layer, rank]
-        return [remote(here, here, sems(layer, 1, t), across(t)) for t in range(1, others)]
+        return [remote(here, here, sems(layer, 1), across(t)) for t in range(1, others)]
 
     def collect(layer):
         here = s.total_v.at[layer, piece(mine)]
-        return [remote(here, here, sems(layer, 2, t), in_group(t)) for t in range(1, group)]
+        return [remote(here, here, sems(layer, 2), in_group(t)) for t in range(1, group)]
+
+    def stage_bytes(layer, stage):
+        here = (
+            s.part.at[layer, pl.ds(0, group - 1)],
+            s.part_sum.at[layer, pl.ds(0, others - 1)],
+            s.total_v.at[layer, pl.ds(0, 8 * (group - 1))],
+        )[stage]
+        return remote(here, here, sems(layer, stage), in_group(1))
 
     def start(copies):
         for copy in copies:
             copy.start()
 
-    def wait(copies):
-        for copy in copies:
-            copy.wait()
-
     def reduce_start(layer):
         start(scatter(layer))
         s.part[layer, mine] = s.packed[layer, piece(mine), :]
 
     def reduce_middle(layer):
-        wait(scatter(layer))
+        stage_bytes(layer, 0).wait()
         value = s.part[layer, 0]
         for t in range(1, group):
             value = value + s.part[layer, t]
@@ -490,7 +494,7 @@
         start(spread(layer))
 
     def reduce_last(layer):
-        wait(spread(layer))
+        stage_bytes(layer, 1).wait()
         value = s.part_sum[layer, 0]
         for t in range(1, others):
             value = value + s.part_sum[layer, t]
@@ -595,10 +599,6 @@
     with jax.named_scope("cotangent"):
         pulls["cot"].wait()
         traces(s.cot_v, keep_gflux(True))
-    with jax.named_scope("cotangent_far"):
-        s.gflux_f[...] = dot(s.rem_t[...], s.gflux[...]).astype(BF16)
-        for a in range(4):
-            s.ghid_f[:, wide(a)] = hidden_grad(s.gflux_f[:, wide(a)], s.gflux_f[:, high(a)], 1)
     with jax.named_scope("far0"):
         far_pairs(0, 0)
     with jax.named_scope("field1"):
@@ -609,6 +609,10 @@
     with jax.named_scope("pack1"):
         s.sent[1] = gathered(s.sel, s.trace)
     send_all(1, 1)
+    with jax.named_scope("cotangent_far"):
+        s.gflux_f[...] = dot(s.rem_t[...], s.gflux[...]).astype(BF16)
+        for a in range(4):
+            s.ghid_f[:, wide(a)] = hidden_grad(s.gflux_f[:, wide(a)], s.gflux_f[:, high(a)], 1)
     with jax.named_scope("near1"):
         s.raw[...] = gathered(s.loc, s.trace)
         far_inner(1)
@@ -650,7 +654,7 @@
         pack_grads(1, one + s.one[...], two + s.two[...], row + s.row[0:1, :])
         reduce_start(1)
     with jax.named_scope("wait2"):
-        wait_all(2, -1)
+        all_of(2).wait_recv()
     with jax.named_scope("grad1"):
         h, l = split(s.got[2])
         s.gin[...] += dot(s.sel_t[...], h) + dot(s.sel_t[...], l)
@@ -659,6 +663,8 @@
         traces(s.grad, keep_gflux(False))
     with jax.named_scope("back0"):
         back_near(0, s.gflux)
+    with jax.named_scope("sum1a"):
+        reduce_middle(1)
     with jax.named_scope("weight_grads0"):
         parts = s.pair_nh.at[0], s.pair_nl.at[0], s.gpre_nh, s.gpre_nl, s.hid_nh.at[0], s.hid_nl.at[0], s.gflux
         pack_grads(0, *weight_grads(parts))
@@ -667,11 +673,9 @@
         turn_back_near()
     with jax.named_scope("pack3"):
         s.sent[3] = gathered(s.rem_t, s.turn)
-    send_all(3, -1)
-    with jax.named_scope("sum1a"):
-        reduce_middle(1)
     with jax.named_scope("sum0a"):
         reduce_middle(0)
+    send_all(3, -1)
     with jax.named_scope("scatter0"):
         both = dot(s.loc_t[...], s.turn[...])
         s.gin[...] += both[:, 0:512] + both[:, 512:1024]
@@ -682,7 +686,7 @@
     with jax.named_scope("sum0b"):
         reduce_last(0)
     with jax.named_scope("wait3"):
-        wait_all(3, -1)
+        all_of(3).wait_recv()
     with jax.named_scope("grad0"):
         h, l = split(s.got[3])
         s.gin[...] += dot(s.sel_t[...], h) + dot(s.sel_t[...], l)
@@ -692,15 +696,16 @@
         push = pltpu.make_async_copy(s.out_v, s.out, s.out_sem.at[0])
         push.start()
     with jax.named_scope("sumc"):
-        wait(collect(1))
-        wait(collect(0))
+        stage_bytes(1, 2).wait()
+        stage_bytes(0, 2).wait()
         push_total = pltpu.make_async_copy(s.total_v, s.total, s.out_sem.at[1])
         push_total.start()
     with jax.named_scope("sent"):
-        wait_sent(0, 1)
-        wait_sent(1, 1)
-        wait_sent(2, -1)
-        wait_sent(3, -1)
+        for which in (0, 1):
+            drain = pltpu.make_async_copy(s.sent.at[which], s.sent.at[which], s.send_sem.at[which])
+            drain.wait()
+        all_of(2).wait_send()
+        all_of(3).wait_send()
         push.wait()
         push_total.wait()
 
@@ -730,10 +735,11 @@
         live_v=pltpu.SMEM((1,), I32),
         out_sem=pltpu.SemaphoreType.DMA((2,)),
         in_sem=pltpu.SemaphoreType.DMA((11,)),
-        send_sem=pltpu.SemaphoreType.DMA((4, BLOCKS)),
-        recv_sem=pltpu.SemaphoreType.DMA((4, BLOCKS)),
-        ar_send=pltpu.SemaphoreType.DMA((2, 3, 16)),
-        ar_recv=pltpu.SemaphoreType.DMA((2, 3, 16)),
+        send_sem=pltpu.SemaphoreType.DMA((4,)),
+        near_sem=pltpu.SemaphoreType.DMA((2, NEIGH)),
+        back_sem=pltpu.SemaphoreType.DMA((2,)),
+        ar_send=pltpu.SemaphoreType.DMA((2, 3)),
+        ar_recv=pltpu.SemaphoreType.DMA((2, 3)),
     )
     names += list(extra)
     scratch += list(extra.values())

time: 62.7 us -> 60.7 us (0.968); the launches traced: 61.5 us -> 60.5 us
  Pallas kernels: 60.2 us -> 59.2 us
    pallas_call x1, Pallas kernels: 58.4 us -> 57.4 us  [local(): pl.pallas_call(functools.partial(kernel, count, names), out_shape=(jax.Sh...]
where the time goes in v3:
time: 60.7 us; the launch traced here: 60.5 us
  Pallas kernels  59.2 us (98%)
  between operations  1.29 us (2%)
    pallas_call x1, Pallas kernels, local(): pl.pallas_call(functools.partial(kernel, count, names), out_shape=(jax.Sh...  57.4 us
    pallas_call x1, Pallas kernels, local(): pl.pallas_call(functools.partial(finish, factor), out_shape=(jax.ShapeDty...  1.82 us

profile of v3, /device:TPU:0, one launch (start us, length us, event | category | flops | bytes accessed | tf_op | source)
XLA Modules:
  0.0 60.5 jit_solution(5073703200479935586)
XLA Ops:
  1.3 57.4 %shard_map.138 = (f32[48,2048]{1,0:T(8,128)}, f32[2,64,128]{2,1,0:T(8,128)}) custom-call(f32[48,2048]{1,0:T(8,128)} %refs_0_.1, f32[48,2048]{1,0:T(8,128)} %refs_1_.1, s32[1]{0:T(128)S(6)} %copy.15.refs_2_, s32[288]{0:T(512)} %refs_3_.1, s32[288]{0:T(512)} %refs_4_.1, s32[1,256]{1,0:T(1,128)} %bitcast.4, f32[2,3,32,32]{3,2,1,0:T(8,128)} %refs_6_.1, ...), custom_call_target="tpu_custom_call" | custom-call | tf_op jit(solution)/shard_map/pallas_call | solution.py:746
  58.7 1.8 %shard_map.139 = (f32[48,2048]{1,0:T(8,128)}, f32[2,64,64]{2,1,0:T(8,128)}, f32[2,64]{1,0:T(2,128)}, f32[2,32,64]{2,1,0:T(8,128)}) custom-call(f32[2,64,128]{2,1,0:T(8,128)} %get-tuple-element.10.total_ref, f32[48,2048]{1,0:T(8,128)} %get-tuple-element.11.field_ref), custom_call_target="tpu_custom_call" | custom-call | tf_op jit(solution)/shard_map/pallas_call | solution.py:760

commit v4 on v3

--- a/solution.py
+++ b/solution.py
@@ -132,13 +132,12 @@
     partners = [neighbour(o) for o in OFFSETS]
     partners += [in_group(step) for step in range(1, group)]
     partners += [across(step) for step in range(1, others)]
-    for device in partners:
-        pl.semaphore_signal(barrier, inc=1, device_id=(device,), device_id_type=MESH)
-
     pulls = {}
     for n, name in enumerate(("send", "state", "live", "src", "orient", "vol", "w1", "b1", "w2t", "deriv", "cot")):
         pulls[name] = pltpu.make_async_copy(getattr(s, name), getattr(s, name + "_v"), s.in_sem.at[n])
         pulls[name].start()
+    for device in partners:
+        pl.semaphore_signal(barrier, inc=1, device_id=(device,), device_id_type=MESH)
 
     def far_copy(which, pair, side, sign):
         rows = pl.ds(pl.multiple_of(64 * pair + CAP * side, CAP), CAP)
@@ -152,8 +151,8 @@
             device_id_type=MESH,
         )
 
-    def send_all(which, sign):
-        for pair in (3, 2, 1, 0):
+    def send_all(which, sign, pairs=(3, 2, 1, 0)):
+        for pair in pairs:
             for side in range(2):
                 far_copy(which, pair, side, sign).start()
 
@@ -663,19 +662,20 @@
         traces(s.grad, keep_gflux(False))
     with jax.named_scope("back0"):
         back_near(0, s.gflux)
-    with jax.named_scope("sum1a"):
-        reduce_middle(1)
     with jax.named_scope("weight_grads0"):
         parts = s.pair_nh.at[0], s.pair_nl.at[0], s.gpre_nh, s.gpre_nl, s.hid_nh.at[0], s.hid_nl.at[0], s.gflux
         pack_grads(0, *weight_grads(parts))
         reduce_start(0)
+    with jax.named_scope("sum1a"):
+        reduce_middle(1)
     with jax.named_scope("turn0"):
         turn_back_near()
     with jax.named_scope("pack3"):
         s.sent[3] = gathered(s.rem_t, s.turn)
+    send_all(3, -1, (3,))
     with jax.named_scope("sum0a"):
         reduce_middle(0)
-    send_all(3, -1)
+    send_all(3, -1, (2, 1, 0))
     with jax.named_scope("scatter0"):
         both = dot(s.loc_t[...], s.turn[...])
         s.gin[...] += both[:, 0:512] + both[:, 512:1024]

time: 60.7 us -> 59.1 us (0.974)
  Pallas kernels: 59.2 us -> 57.6 us
    pallas_call x1, Pallas kernels: 57.4 us -> 55.8 us  [local(): pl.pallas_call(functools.partial(kernel, count, names), out_shape=(jax.Sh...]
where the time goes in v4:
time: 59.1 us; the launch traced here: 58.9 us
  Pallas kernels  57.6 us (97%)
  between operations  1.29 us (2%)
    pallas_call x1, Pallas kernels, local(): pl.pallas_call(functools.partial(kernel, count, names), out_shape=(jax.Sh...  55.8 us
    pallas_call x1, Pallas kernels, local(): pl.pallas_call(functools.partial(finish, factor), out_shape=(jax.ShapeDty...  1.82 us

profile of v4, /device:TPU:0, one launch (start us, length us, event | category | flops | bytes accessed | tf_op | source)
XLA Modules:
  0.0 58.9 jit_solution(4496913268720629241)
XLA Ops:
  1.3 55.8 %shard_map.138 = (f32[48,2048]{1,0:T(8,128)}, f32[2,64,128]{2,1,0:T(8,128)}) custom-call(f32[48,2048]{1,0:T(8,128)} %refs_0_.1, f32[48,2048]{1,0:T(8,128)} %refs_1_.1, s32[1]{0:T(128)S(6)} %copy.15.refs_2_, s32[288]{0:T(512)} %refs_3_.1, s32[288]{0:T(512)} %refs_4_.1, s32[1,256]{1,0:T(1,128)} %bitcast.4, f32[2,3,32,32]{3,2,1,0:T(8,128)} %refs_6_.1, ...), custom_call_target="tpu_custom_call" | custom-call | tf_op jit(solution)/shard_map/pallas_call | solution.py:746
  57.1 1.8 %shard_map.139 = (f32[48,2048]{1,0:T(8,128)}, f32[2,64,64]{2,1,0:T(8,128)}, f32[2,64]{1,0:T(2,128)}, f32[2,32,64]{2,1,0:T(8,128)}) custom-call(f32[2,64,128]{2,1,0:T(8,128)} %get-tuple-element.10.total_ref, f32[48,2048]{1,0:T(8,128)} %get-tuple-element.11.field_ref), custom_call_target="tpu_custom_call" | custom-call | tf_op jit(solution)/shard_map/pallas_call | solution.py:760

commit v5 on v4

--- a/solution.py
+++ b/solution.py
@@ -105,6 +105,7 @@
     w2c=((2, 256, 256), BF16), w2ts=((2, 256, 256), BF16), w2tl=((2, 128, 256), BF16),
     vs=((2, 256, 384), BF16), vl=((2, 128, 384), BF16), vts=((2, 256, 384), BF16), vtl=((2, 128, 384), BF16), bias=((2, 8, 256), F32),
     sent=((4, SLOTS, 512), F32), got=((4, SLOTS, 512), F32),
+    slope=((FACES, 1024), F32),
     one=((256, 256), F32), two=((256, 128), F32), row=((8, 256), F32),
     packed=((2, 64, 128), F32), part=((2, 8, 8, 128), F32),
 )
@@ -140,7 +141,7 @@
         pl.semaphore_signal(barrier, inc=1, device_id=(device,), device_id_type=MESH)
 
     def far_copy(which, pair, side, sign):
-        rows = pl.ds(pl.multiple_of(64 * pair + CAP * side, CAP), CAP)
+        rows = pl.ds(64 * pair + CAP * side, CAP)
         offset = (pair + 1) * (sign if side == 0 else -sign)
         return pltpu.make_async_remote_copy(
             src_ref=s.sent.at[which, rows],
@@ -157,7 +158,7 @@
                 far_copy(which, pair, side, sign).start()
 
     def all_of(which, pair=None):
-        rows = pl.ds(0, SLOTS) if pair is None else pl.ds(pl.multiple_of(64 * pair, 64), 64)
+        rows = pl.ds(0, SLOTS) if pair is None else pl.ds(64 * pair, 64)
         return pltpu.make_async_remote_copy(
             src_ref=s.sent.at[which, rows],
             dst_ref=s.got.at[which, rows],
@@ -343,7 +344,10 @@
 
     def hidden_near(layer):
         def body(w, h_, n):
-            h, l = split(hidden(s.pair_nh[layer, :, w], s.pair_nl[layer, :, w], layer))
+            value = hidden(s.pair_nh[layer, :, w], s.pair_nl[layer, :, w], layer)
+            h, l = split(value)
+            if layer == 1:
+                s.slope[:, w] = 1.0 - value * value
             s.hid_nh[layer, :, w] = h
             s.hid_nl[layer, :, w] = l
             if layer == 0:
@@ -353,24 +357,25 @@
 
     def back_near(layer, gflux):
         def body(w, h_, n):
-            h = s.hid_nh[layer, :, w].astype(F32) + s.hid_nl[layer, :, w].astype(F32)
-            gp = hidden_grad(gflux[:, w], gflux[:, h_], layer) * (1.0 - h * h)
-            gh, gl = split(gp)
-            s.gpre_nh[:, w] = gh
-            s.gpre_nl[:, w] = gl
-            both = pair_grad(gh, gl, layer)
+            gp = hidden_grad(gflux[:, w], gflux[:, h_], layer) * s.slope[:, w]
+            s.gpre_nh[:, w], s.gpre_nl[:, w] = split(gp)
+
+        each_a(body)
+
+    def back_pair(layer):
+        def body(w, h_, n):
+            both = pair_grad(s.gpre_nh[:, w], s.gpre_nl[:, w], layer)
             s.gin[:, n] = both[:, 0:128]
             s.gout[:, n] = both[:, 128:256]
 
         each_a(body)
 
     def far_pairs(which, layer):
-        def step(n, carry):
-            pair = 3 - n
-            rows = pl.ds(pl.multiple_of(64 * pair, 64), 64)
+        def step(pair):
+            rows = pl.ds(64 * pair, 64)
             all_of(which, pair).wait_recv()
             for side in range(2):
-                part_rows = pl.ds(pl.multiple_of(64 * pair + CAP * side, CAP), CAP)
+                part_rows = pl.ds(64 * pair + CAP * side, CAP)
                 x = oriented([s.got[which, part_rows, narrow(a)] for a in range(4)], marks_of(s.masks_f, part_rows))
                 for a in range(4):
                     s.pair_fh[layer, part_rows, low(a)], s.pair_fl[layer, part_rows, low(a)] = split(x[a])
@@ -396,16 +401,16 @@
                     s.gin_fh[rows, narrow(a)] = part_of(ih, a)
                     s.gin_fl[rows, narrow(a)] = part_of(il, a)
                 for side in range(2):
-                    part_rows = pl.ds(pl.multiple_of(64 * pair + CAP * side, CAP), CAP)
+                    part_rows = pl.ds(64 * pair + CAP * side, CAP)
                     cut = lambda a: both[64 * a + CAP * side : 64 * a + CAP * side + CAP, 128:256]
                     x = turned_back([cut(a) for a in range(4)], marks_of(s.masks_f, part_rows))
                     for a in range(4):
                         s.sent[which + 1, part_rows, narrow(a)] = x[a]
                 for side in range(2):
                     far_copy(which + 1, pair, side, -1).start()
-            return carry
-
-        lax.fori_loop(0, 4, step, 0)
+
+        for pair in (3, 2, 1, 0):
+            step(pair)
 
     def far_inner(layer):
         both = dot(s.rem_t[...], s.trace[...]).astype(BF16)
@@ -465,14 +470,14 @@
         return [remote(here, here, sems(layer, 1), across(t)) for t in range(1, others)]
 
     def collect(layer):
-        here = s.total_v.at[layer, piece(mine)]
-        return [remote(here, here, sems(layer, 2), in_group(t)) for t in range(1, group)]
+        here, there = s.total_v.at[layer, piece(mine)], s.total.at[layer, piece(mine)]
+        return [remote(here, there, sems(layer, 2), in_group(t)) for t in range(1, group)]
 
     def stage_bytes(layer, stage):
         here = (
             s.part.at[layer, pl.ds(0, group - 1)],
             s.part_sum.at[layer, pl.ds(0, others - 1)],
-            s.total_v.at[layer, pl.ds(0, 8 * (group - 1))],
+            s.total.at[layer, pl.ds(0, 8 * (group - 1))],
         )[stage]
         return remote(here, here, sems(layer, stage), in_group(1))
 
@@ -492,6 +497,11 @@
         s.part_sum[layer, rank] = value
         start(spread(layer))
 
+    def push_piece(layer):
+        return pltpu.make_async_copy(
+            s.total_v.at[layer, piece(mine)], s.total.at[layer, piece(mine)], s.out_sem.at[1 + layer]
+        )
+
     def reduce_last(layer):
         stage_bytes(layer, 1).wait()
         value = s.part_sum[layer, 0]
@@ -499,6 +509,7 @@
             value = value + s.part_sum[layer, t]
         s.total_v[layer, piece(mine), :] = value
         start(collect(layer))
+        push_piece(layer).start()
 
     with jax.named_scope("send_table"):
         order = (0, 4, 1, 5, 2, 6, 3, 7)
@@ -517,11 +528,15 @@
         for n in range(16):
             s.field[:, narrow(n)] = jnp.where(alive, tile(s.state_v, n), 0.0)
         traces(s.field, keep_traces(0))
+    far_half, close_half = slice(128, 256), slice(0, 128)
     with jax.named_scope("pack0"):
-        s.sent[0] = gathered(s.sel, s.trace)
+        s.sent[0, far_half] = gathered(s.sel.at[far_half], s.trace)
     with jax.named_scope("barrier"):
         pl.semaphore_wait(barrier, len(partners))
-    send_all(0, 1)
+    send_all(0, 1, (3, 2))
+    with jax.named_scope("pack0b"):
+        s.sent[0, close_half] = gathered(s.sel.at[close_half], s.trace)
+    send_all(0, 1, (1, 0))
 
     with jax.named_scope("tables"):
         for f in range(6):
@@ -606,8 +621,11 @@
             s.field[:, narrow(n)] += STEP_SIZE * (lift(s.flux, n // 4, n % 4) - s.volume[:, narrow(n)])
         traces(s.field, keep_traces(1))
     with jax.named_scope("pack1"):
-        s.sent[1] = gathered(s.sel, s.trace)
-    send_all(1, 1)
+        s.sent[1, far_half] = gathered(s.sel.at[far_half], s.trace)
+    send_all(1, 1, (3, 2))
+    with jax.named_scope("pack1b"):
+        s.sent[1, close_half] = gathered(s.sel.at[close_half], s.trace)
+    send_all(1, 1, (1, 0))
     with jax.named_scope("cotangent_far"):
         s.gflux_f[...] = dot(s.rem_t[...], s.gflux[...]).astype(BF16)
         for a in range(4):
@@ -621,6 +639,7 @@
         hidden_near(1)
     with jax.named_scope("back1"):
         back_near(1, s.gflux_n)
+        back_pair(1)
     with jax.named_scope("whole0"):
         for far, here in ((s.pair_fh, s.pair_nh), (s.pair_fl, s.pair_nl)):
             value = dot(s.rem[...], jnp.concatenate([far[0, :, low(a)] for a in range(4)], axis=1)).astype(BF16)
@@ -652,6 +671,10 @@
         one, two, row = weight_grads(parts)
         pack_grads(1, one + s.one[...], two + s.two[...], row + s.row[0:1, :])
         reduce_start(1)
+    with jax.named_scope("slope0"):
+        for a in range(4):
+            h = s.hid_nh[0, :, wide(a)].astype(F32) + s.hid_nl[0, :, wide(a)].astype(F32)
+            s.slope[:, wide(a)] = 1.0 - h * h
     with jax.named_scope("wait2"):
         all_of(2).wait_recv()
     with jax.named_scope("grad1"):
@@ -668,11 +691,15 @@
         reduce_start(0)
     with jax.named_scope("sum1a"):
         reduce_middle(1)
+    with jax.named_scope("back0_pair"):
+        back_pair(0)
     with jax.named_scope("turn0"):
         turn_back_near()
     with jax.named_scope("pack3"):
-        s.sent[3] = gathered(s.rem_t, s.turn)
+        s.sent[3, far_half] = gathered(s.rem_t.at[far_half], s.turn)
     send_all(3, -1, (3,))
+    with jax.named_scope("pack3b"):
+        s.sent[3, close_half] = gathered(s.rem_t.at[close_half], s.turn)
     with jax.named_scope("sum0a"):
         reduce_middle(0)
     send_all(3, -1, (2, 1, 0))
@@ -698,8 +725,6 @@
     with jax.named_scope("sumc"):
         stage_bytes(1, 2).wait()
         stage_bytes(0, 2).wait()
-        push_total = pltpu.make_async_copy(s.total_v, s.total, s.out_sem.at[1])
-        push_total.start()
     with jax.named_scope("sent"):
         for which in (0, 1):
             drain = pltpu.make_async_copy(s.sent.at[which], s.sent.at[which], s.send_sem.at[which])
@@ -707,7 +732,8 @@
         all_of(2).wait_send()
         all_of(3).wait_send()
         push.wait()
-        push_total.wait()
+        push_piece(1).wait()
+        push_piece(0).wait()
 
 
 def finish(factor, total_ref, field_ref, out_ref, w1_ref, b1_ref, w2t_ref):
@@ -733,7 +759,7 @@
         part_sum=pltpu.VMEM((2, count // 8, 8, 128), F32),
         total_v=pltpu.VMEM((2, 64, 128), F32),
         live_v=pltpu.SMEM((1,), I32),
-        out_sem=pltpu.SemaphoreType.DMA((2,)),
+        out_sem=pltpu.SemaphoreType.DMA((3,)),
         in_sem=pltpu.SemaphoreType.DMA((11,)),
         send_sem=pltpu.SemaphoreType.DMA((4,)),
         near_sem=pltpu.SemaphoreType.DMA((2, NEIGH)),

time: 59.1 us -> 58.4 us (0.988)
  Pallas kernels: 57.6 us -> 57 us
    pallas_call x1, Pallas kernels: 55.8 us -> 55.2 us  [local(): pl.pallas_call(functools.partial(kernel, count, names), out_shape=(jax.Sh...]
where the time goes in v5:
time: 58.4 us; the launch traced here: 58.3 us
  Pallas kernels  57 us (98%)
  between operations  1.29 us (2%)
    pallas_call x1, Pallas kernels, local(): pl.pallas_call(functools.partial(kernel, count, names), out_shape=(jax.Sh...  55.2 us
    pallas_call x1, Pallas kernels, local(): pl.pallas_call(functools.partial(finish, factor), out_shape=(jax.ShapeDty...  1.82 us

profile of v5, /device:TPU:0, one launch (start us, length us, event | category | flops | bytes accessed | tf_op | source)
XLA Modules:
  0.0 58.3 jit_solution(5431835789311680756)
XLA Ops:
  1.3 55.2 %shard_map.138 = (f32[48,2048]{1,0:T(8,128)}, f32[2,64,128]{2,1,0:T(8,128)}) custom-call(f32[48,2048]{1,0:T(8,128)} %refs_0_.1, f32[48,2048]{1,0:T(8,128)} %refs_1_.1, s32[1]{0:T(128)S(6)} %copy.15.refs_2_, s32[288]{0:T(512)} %refs_3_.1, s32[288]{0:T(512)} %refs_4_.1, s32[1,256]{1,0:T(1,128)} %bitcast.4, f32[2,3,32,32]{3,2,1,0:T(8,128)} %refs_6_.1, ...), custom_call_target="tpu_custom_call" | custom-call | tf_op jit(solution)/shard_map/pallas_call | solution.py:772
  56.5 1.8 %shard_map.139 = (f32[48,2048]{1,0:T(8,128)}, f32[2,64,64]{2,1,0:T(8,128)}, f32[2,64]{1,0:T(2,128)}, f32[2,32,64]{2,1,0:T(8,128)}) custom-call(f32[2,64,128]{2,1,0:T(8,128)} %get-tuple-element.10.total_ref, f32[48,2048]{1,0:T(8,128)} %get-tuple-element.11.field_ref), custom_call_target="tpu_custom_call" | custom-call | tf_op jit(solution)/shard_map/pallas_call | solution.py:786

commit v6 on v5

--- a/solution.py
+++ b/solution.py
@@ -693,11 +693,17 @@
         reduce_middle(1)
     with jax.named_scope("back0_pair"):
         back_pair(0)
+    with jax.named_scope("pack3"):
+        h, l = split(s.gout[...])
+        s.turn[:, 0:512] = h
+        s.turn[:, 512:1024] = l
+        value = gathered(s.rem_t.at[far_half], s.turn)
+        x = turned_back([value[:, narrow(a)] for a in range(4)], marks_of(s.masks_f, far_half))
+        for a in range(4):
+            s.sent[3, far_half, narrow(a)] = x[a]
+    send_all(3, -1, (3,))
     with jax.named_scope("turn0"):
         turn_back_near()
-    with jax.named_scope("pack3"):
-        s.sent[3, far_half] = gathered(s.rem_t.at[far_half], s.turn)
-    send_all(3, -1, (3,))
     with jax.named_scope("pack3b"):
         s.sent[3, close_half] = gathered(s.rem_t.at[close_half], s.turn)
     with jax.named_scope("sum0a"):

time: 58.4 us -> 58.2 us (level)
  no operation moved by 1% of the time
where the time goes in v6:
time: 58.2 us; the launch traced here: 58.1 us
  Pallas kernels  56.8 us (98%)
  between operations  1.29 us (2%)
    pallas_call x1, Pallas kernels, local(): pl.pallas_call(functools.partial(kernel, count, names), out_shape=(jax.Sh...  55 us
    pallas_call x1, Pallas kernels, local(): pl.pallas_call(functools.partial(finish, factor), out_shape=(jax.ShapeDty...  1.82 us

profile of v6, /device:TPU:0, one launch (start us, length us, event | category | flops | bytes accessed | tf_op | source)
XLA Modules:
  0.0 58.1 jit_solution(5503244976703545306)
XLA Ops:
  1.3 55.0 %shard_map.138 = (f32[48,2048]{1,0:T(8,128)}, f32[2,64,128]{2,1,0:T(8,128)}) custom-call(f32[48,2048]{1,0:T(8,128)} %refs_0_.1, f32[48,2048]{1,0:T(8,128)} %refs_1_.1, s32[1]{0:T(128)S(6)} %copy.15.refs_2_, s32[288]{0:T(512)} %refs_3_.1, s32[288]{0:T(512)} %refs_4_.1, s32[1,256]{1,0:T(1,128)} %bitcast.4, f32[2,3,32,32]{3,2,1,0:T(8,128)} %refs_6_.1, ...), custom_call_target="tpu_custom_call" | custom-call | tf_op jit(solution)/shard_map/pallas_call | solution.py:778
  56.2 1.8 %shard_map.139 = (f32[48,2048]{1,0:T(8,128)}, f32[2,64,64]{2,1,0:T(8,128)}, f32[2,64]{1,0:T(2,128)}, f32[2,32,64]{2,1,0:T(8,128)}) custom-call(f32[2,64,128]{2,1,0:T(8,128)} %get-tuple-element.10.total_ref, f32[48,2048]{1,0:T(8,128)} %get-tuple-element.11.field_ref), custom_call_target="tpu_custom_call" | custom-call | tf_op jit(solution)/shard_map/pallas_call | solution.py:792
